TPU v7x, 32 devices: a whole 2x2x4 slice. The times are simulated.
32 devices in a mesh: groups: 2 (over x), dev: 16 (over z, y, core).
Axes of the slice: x: 2, y: 2, z: 4, core: 2. Of those that a mesh axis runs over, the one named last changes fastest.
Arguments:
- hidden_in: bfloat16 [512, 4096], P(('groups', 'dev')), parts along dimension 0, may hold values from -2 to 2
- queries: bfloat16 [512, 4096], P(('groups', 'dev')), parts along dimension 0, may hold values from -80 to 80
- fresh_key_value: bfloat16 [512, 2, 256], P(('groups', 'dev')), parts along dimension 0, may hold values from -6 to 6
- segment_key_cache: bfloat16 [4096, 16, 256], P(('groups', 'dev')), parts along dimension 0, may hold values from -6 to 6
- segment_value_cache: bfloat16 [4096, 16, 256], P(('groups', 'dev')), parts along dimension 0, may hold values from -6 to 6
- segment_owner_row: int32 [4096], P(('groups', 'dev')), parts along dimension 0, may hold values from 0 to 255, as said below
- segment_length: int32 [4096], P(('groups', 'dev')), parts along dimension 0, may hold values from 1 to 16
- expert_ids: int32 [512, 8], P(('groups', 'dev')), parts along dimension 0, may hold values from 0 to 15, all different within a row; in each aligned block of 16 rows (0 to 15, 16 to 31, ...) at most 8 rows name the same one
- gate_score: int32 [512, 8], P(('groups', 'dev')), parts along dimension 0, may hold values from 0 to 11
- out_proj: bfloat16 [4096, 4096], P('dev'), may hold values from -0.09375 to 0.09375
- norm_gain: bfloat16 [4096], replicated, may hold values from 0.099609375 to 1.8984375
- w_gate: bfloat16 [16, 4096, 768], P('dev'), may hold values from -0.09375 to 0.09375
- w_up: bfloat16 [16, 4096, 768], P('dev'), may hold values from -0.09375 to 0.09375
- w_down: bfloat16 [16, 768, 4096], P('dev'), may hold values from -0.21875 to 0.21875
Outputs:
- layer_out: bfloat16 [512, 4096], P(('groups', 'dev')), parts along dimension 0
There are 2 independent parts, one for each index of `groups`. A program takes and returns all parts, laid end to end along the dimension named above; an argument that names none is the same for every part. Nothing has to cross between parts.
Inputs may be any that keep to these rules, and one draw needn't show every extreme that they name: `segment_owner_row`: segment rows never fall along the segments, and every row owns at least one segment. `expert_ids`: each row names 8 different experts; among the rows of one device no expert is named by more than 8 rows.
All inputs are finite; a program needn't handle non-finite values.
Results may differ from a plain program's by a relative error of at most 0.024.
Values may be sent and summed in bfloat16 or wider, within the bound.
A program may use at most 128 MiB of HBM per device.

v0:
```python
import jax
import jax.numpy as jnp
from jax import lax
from jax.sharding import PartitionSpec as P

HEAD_SIZE = 128
TOP = 8
HQ = 32


def segment_terms(query_rows, key_cache, value_cache, seg_lengths):
    seg_count = key_cache.shape[0]
    seg_width = key_cache.shape[1]
    kv_heads = key_cache.shape[2] // HEAD_SIZE
    group_size = HQ // kv_heads
    query_blocks = query_rows.reshape(seg_count, kv_heads, group_size, HEAD_SIZE)
    key_blocks = key_cache.reshape(seg_count, seg_width, kv_heads, HEAD_SIZE)
    value_blocks = value_cache.reshape(seg_count, seg_width, kv_heads, HEAD_SIZE)
    scores = jnp.einsum(
        "skgd,stkd->skgt", query_blocks, key_blocks, preferred_element_type=jnp.float32
    ) * HEAD_SIZE ** (-0.5)
    live_slots = (
        jnp.arange(seg_width, dtype=jnp.int32)[None, None, None, :]
        < seg_lengths[:, None, None, None]
    )
    scores = jnp.where(live_slots, scores, -jnp.inf)
    seg_max = jnp.max(scores, axis=3)
    prob_rows = jnp.exp(scores - seg_max[..., None])
    seg_sum = jnp.sum(prob_rows, axis=3)
    seg_out = jnp.einsum(
        "skgt,stkd->skgd",
        prob_rows.astype(jnp.bfloat16),
        value_blocks,
        preferred_element_type=jnp.float32,
    )
    return (
        seg_max.reshape(seg_count, HQ),
        seg_sum.reshape(seg_count, HQ),
        seg_out.reshape(seg_count, HQ, HEAD_SIZE),
    )


def reduce_rows(seg_max, seg_sum, seg_out, row_ids, row_count):
    row_max = jax.ops.segment_max(seg_max, row_ids, num_segments=row_count)
    weight = jnp.exp(seg_max - jnp.take(row_max, row_ids, axis=0))
    row_sum = jax.ops.segment_sum(seg_sum * weight, row_ids, num_segments=row_count)
    row_out = jax.ops.segment_sum(seg_out * weight[..., None], row_ids, num_segments=row_count)
    return (row_max, row_sum, row_out)


def fold_own(row_max, row_sum, row_out, query_own, kv_own):
    row_count = query_own.shape[0]
    kv_heads = kv_own.shape[2] // HEAD_SIZE
    group_size = HQ // kv_heads
    query_blocks = query_own.reshape(row_count, kv_heads, group_size, HEAD_SIZE).astype(jnp.float32)
    new_key = kv_own[:, 0].reshape(row_count, kv_heads, 1, HEAD_SIZE).astype(jnp.float32)
    new_value = kv_own[:, 1].reshape(row_count, kv_heads, 1, HEAD_SIZE).astype(jnp.float32)
    own_score = jnp.sum(query_blocks * new_key, axis=3).reshape(row_count, HQ) * HEAD_SIZE ** (-0.5)
    merged = jnp.maximum(row_max, own_score)
    old_weight = jnp.exp(row_max - merged)
    new_weight = jnp.exp(own_score - merged)
    total_sum = row_sum * old_weight + new_weight
    value_term = jnp.broadcast_to(new_value, (row_count, kv_heads, group_size, HEAD_SIZE)).reshape(
        row_count, HQ, HEAD_SIZE
    )
    merged_out = row_out * old_weight[..., None] + value_term * new_weight[..., None]
    return (merged, total_sum, merged_out)


def finish(row_max, row_sum, row_out):
    floored = jnp.maximum(row_sum, 1.0)
    block_lse = row_max + jnp.log(floored)
    block_share = (row_out / floored[..., None]).astype(jnp.bfloat16)
    return (block_lse, block_share)


def on_device(
    hidden_in,
    queries,
    fresh_key_value,
    segment_key_cache,
    segment_value_cache,
    segment_owner_row,
    segment_length,
    expert_ids,
    gate_score,
    out_proj,
    norm_gain,
    w_gate,
    w_up,
    w_down,
):
    devices = lax.axis_size("dev")
    my_index = lax.axis_index("dev")
    row_dev = hidden_in.shape[0]
    row_total = row_dev * devices
    per_device = HQ // devices
    own_first = my_index * row_dev
    query_all = lax.all_gather(queries, "dev", axis=0, tiled=True)
    query_rows = jnp.take(query_all, segment_owner_row, axis=0)
    seg_max, seg_sum, seg_out = segment_terms(
        query_rows, segment_key_cache, segment_value_cache, segment_length
    )
    row_max, row_sum, row_out = reduce_rows(seg_max, seg_sum, seg_out, segment_owner_row, row_total)
    own_max, own_sum, own_out = fold_own(
        lax.dynamic_slice_in_dim(row_max, own_first, row_dev, 0),
        lax.dynamic_slice_in_dim(row_sum, own_first, row_dev, 0),
        lax.dynamic_slice_in_dim(row_out, own_first, row_dev, 0),
        queries,
        fresh_key_value,
    )
    row_max = lax.dynamic_update_slice_in_dim(row_max, own_max, own_first, 0)
    row_sum = lax.dynamic_update_slice_in_dim(row_sum, own_sum, own_first, 0)
    row_out = lax.dynamic_update_slice_in_dim(row_out, own_out, own_first, 0)
    table_lse, table_share = finish(row_max, row_sum, row_out)
    got_lse = lax.all_to_all(table_lse[None], "dev", split_axis=2, concat_axis=0, tiled=True)
    got_share = lax.all_to_all(table_share[None], "dev", split_axis=2, concat_axis=0, tiled=True)
    best_lse = jnp.max(got_lse, axis=0)
    weight = jnp.exp(got_lse - best_lse[None])
    denominator = jnp.sum(weight, axis=0)
    numerator = jnp.sum(weight[..., None] * got_share.astype(jnp.float32), axis=0)
    attn_local = (
        (numerator / denominator[..., None])
        .astype(jnp.bfloat16)
        .reshape(row_total, per_device * HEAD_SIZE)
    )
    projected = lax.psum_scatter(
        jnp.dot(attn_local, out_proj, preferred_element_type=jnp.float32).astype(jnp.bfloat16),
        "dev",
        scatter_dimension=0,
        tiled=True,
    ).astype(jnp.float32)
    mixed_f32 = (hidden_in.astype(jnp.float32) + projected).astype(jnp.bfloat16).astype(jnp.float32)
    normed = (
        mixed_f32
        * lax.rsqrt(jnp.mean(mixed_f32 * mixed_f32, axis=1, keepdims=True) + 1e-06)
        * norm_gain.astype(jnp.float32)
    ).astype(jnp.bfloat16)
    gate_probs = jnp.exp(gate_score.astype(jnp.float32) / 4.0)
    gate_probs = gate_probs / jnp.sum(gate_probs, axis=1, keepdims=True)
    capacity = row_dev // 2
    slot_total = devices * capacity
    flat_ids = expert_ids.reshape(-1)
    one_hot = (flat_ids[:, None] == jnp.arange(devices, dtype=jnp.int32)[None, :]).astype(jnp.int32)
    slot_rank = jnp.sum((jnp.cumsum(one_hot, axis=0) - one_hot) * one_hot, axis=1)
    slot_index = (flat_ids * capacity + slot_rank).reshape(row_dev, TOP)
    slot_iota = jnp.arange(slot_total, dtype=jnp.int32)
    combine_weights = jnp.sum(
        jnp.where(slot_index[:, :, None] == slot_iota[None, None, :], gate_probs[:, :, None], 0.0),
        axis=1,
    )
    dispatch = jnp.any(slot_index[None, :, :] == slot_iota[:, None, None], axis=2).astype(
        jnp.bfloat16
    )
    outgoing = (
        jnp.dot(dispatch, normed, preferred_element_type=jnp.float32)
        .astype(jnp.bfloat16)
        .reshape(devices, capacity, normed.shape[1])
    )
    arrived = lax.all_to_all(outgoing, "dev", split_axis=0, concat_axis=0, tiled=True)
    sources = arrived.shape[0]
    slot_count = arrived.shape[1]
    flat_tokens = arrived.reshape(sources * slot_count, arrived.shape[2])
    gate_proj = jnp.dot(flat_tokens, w_gate[0], preferred_element_type=jnp.float32)
    up_proj = jnp.dot(flat_tokens, w_up[0], preferred_element_type=jnp.float32)
    activated = (jax.nn.silu(gate_proj) * up_proj).astype(jnp.bfloat16)
    result = jnp.dot(activated, w_down[0], preferred_element_type=jnp.float32).astype(jnp.bfloat16)
    returned = lax.all_to_all(
        result.reshape(sources, slot_count, result.shape[1]),
        "dev",
        split_axis=0,
        concat_axis=0,
        tiled=True,
    )
    moe_sum = jnp.dot(
        combine_weights,
        returned.reshape(slot_total, returned.shape[2]).astype(jnp.float32),
        precision=lax.Precision.HIGHEST,
        preferred_element_type=jnp.float32,
    )
    return (mixed_f32 + moe_sum).astype(jnp.bfloat16)


def solution(mesh):
    placed = (
        P(("groups", "dev"), None),
        P(("groups", "dev"), None),
        P(("groups", "dev"), None, None),
        P(("groups", "dev"), None, None),
        P(("groups", "dev"), None, None),
        P(("groups", "dev")),
        P(("groups", "dev")),
        P(("groups", "dev"), None),
        P(("groups", "dev"), None),
        P("dev", None),
        P(),
        P("dev", None, None),
        P("dev", None, None),
        P("dev", None, None),
    )
    return jax.shard_map(
        on_device, mesh=mesh, in_specs=placed, out_specs=P(("groups", "dev"), None), check_vma=False
    )
```

profile of v0, /device:TPU:0, one launch (start us, length us, event | category | flops | bytes accessed | tf_op | source)
XLA Modules:
  0.0 307.8 jit_solution(7378402143327455642)
XLA Ops:
  11.3 42.3 %all-gather.2.cloned.1.call-done = bf16[256,4096]{1,0:T(8,128)(2,1)} async-done(((bf16[16,4096]{1,0:T(8,128)(2,1)}), bf16[256,4096]{1,0:T(8,128)(2,1)}) %all-gather.2.cloned.1.call-update) | async-done | bytes 2097168 | tf_op jit(solution)/shard_map/all_gather | solution.py:99
  53.7 4.1 %gather_fusion = bf16[128,4096]{1,0:T(8,128)(2,1)S(1)} fusion(bf16[256,4096]{1,0:T(8,128)(2,1)} %all-gather.2.cloned.1.call-done, s32[1024]{0:T(1024)S(1)} %pad_clamp_fusion), kind=kCustom, calls=%fused_computation | custom fusion | bytes 2097664 | tf_op jit(solution)/shard_map/jit(_take)/gather | solution.py:100
  58.0 3.3 %fusion.25 = f32[128,2,16,16]{2,3,1,0:T(8,128)} fusion(bf16[128,2,16,128]{3,2,1,0:T(8,128)(2,1)S(1)} %bitcast.96, pred[128]{0:T(512)(128)(4,1)S(1)} %compare_and_fusion, bf16[128,16,256]{2,1,0:T(8,128)(2,1)} %param.17), kind=kOutput, calls=%fused_computation.28 | convolution fusion | flops 17301504 | bytes 2359424 | tf_op jit(solution)/shard_map/skgd,stkd->skgt/dot_general | solution.py:19
  61.3 2.7 copy.115
  65.8 1.6 scatter_custom_fusion
  73.5 3.5 %all-to-all-start = ((f32[1,256,32]{1,0,2:T(1,128)}), f32[1,256,32]{1,0,2:T(1,128)S(1)}, u32[]{:S(2)}, u32[]{:S(2)}) async-start(f32[1,256,32]{1,0,2:T(1,128)} %copy.124), calls=%async_computation | async-start | bytes 65536 | tf_op jit(solution)/shard_map/all_to_all | solution.py:116
  77.0 1.9 fusion.22
  78.9 2.0 bitcast_multiply_fusion.1
  80.9 2.5 broadcast_in_dim.99
  83.4 19.0 %scatter_fusion = f32[256,32,128]{2,1,0:T(8,128)} fusion(f32[256,32,128]{2,1,0:T(8,128)} %broadcast_in_dim.99, s32[128]{0:T(128)S(1)} %copy-done.8, f32[128,32,128]{2,1,0:T(8,128)} %bitcast_multiply_fusion.1), kind=kCustom, calls=%fused_computation.4 | custom fusion | flops 524288 | bytes 6291968 | tf_op jit(solution)/shard_map/scatter-add | solution.py:47
  102.4 1.8 constant_dynamic-update-slice_fusion
  104.2 2.9 fusion.15
  107.1 2.2 copy.128
  109.3 4.7 %all-to-all-start.1 = ((bf16[1,256,32,128]{3,1,0,2:T(8,128)(2,1)}), bf16[1,256,32,128]{3,1,0,2:T(8,128)(2,1)}, u32[]{:S(2)}, u32[]{:S(2)}) async-start(bf16[1,256,32,128]{3,1,0,2:T(8,128)(2,1)} %copy.128), calls=%async_computation.1 | async-start | bytes 4194304 | tf_op jit(solution)/shard_map/all_to_all | solution.py:117
  114.3 40.8 %all-to-all-done.1 = bf16[1,256,32,128]{3,1,0,2:T(8,128)(2,1)} async-done(((bf16[1,256,32,128]{3,1,0,2:T(8,128)(2,1)}), bf16[1,256,32,128]{3,1,0,2:T(8,128)(2,1)}, u32[]{:S(2)}, u32[]{:S(2)}) %all-to-all-start.1) | async-done | bytes 2097184 | tf_op jit(solution)/shard_map/all_to_all | solution.py:117
  155.1 2.5 fusion.14
  157.9 2.1 convolution_convert_fusion
  160.9 67.4 %reduce-scatter.2.cloned.1.call-done = bf16[16,4096]{1,0:T(8,128)(2,1)} async-done(((bf16[256,4096]{1,0:T(8,128)(2,1)}), bf16[16,4096]{1,0:T(8,128)(2,1)}) %reduce-scatter.2.cloned.1.call-update) | async-done | bytes 131088 | tf_op jit(solution)/shard_map/reduce_scatter | solution.py:127
  230.7 28.3 %all_to_all.37 = bf16[16,8,4096]{2,1,0:T(8,128)(2,1)S(1)} all-to-all(bf16[16,8,4096]{2,1,0:T(8,128)(2,1)S(1)} %fusion.9), channel_id=1, replica_groups=mesh['groups'=2,'dev'=16] {'dev'}, dimensions={0} | all-to-all | bytes 2097152 | tf_op jit(solution)/shard_map/all_to_all | solution.py:160
  259.0 3.8 %fusion.4 = f32[128,768]{1,0:T(8,128)S(1)} fusion(bf16[1,4096,768]{2,1,0:T(8,128)(2,1)} %param.25, bf16[16,8,4096]{2,1,0:T(8,128)(2,1)S(1)} %all_to_all.37), kind=kOutput, calls=%fused_computation.9 | convolution fusion | flops 805306368 | bytes 7733248 | tf_op jit(solution)/shard_map/dot_general | solution.py:164
  262.8 8.1 %fusion.10 = bf16[16,8,4096]{2,1,0:T(8,128)(2,1)} fusion(bf16[1,768,4096]{2,1,0:T(8,128)(2,1)} %param.27, bf16[1,4096,768]{2,1,0:T(8,128)(2,1)} %param.26, bf16[16,8,4096]{2,1,0:T(8,128)(2,1)S(1)} %all_to_all.37, f32[128,768]{1,0:T(8,128)S(1)} %fusion.4), kind=kOutput, calls=%fused_computation.15 | convolution fusion | flops 1611726848 | bytes 15073280 | tf_op jit(solution)/shard_map/dot_general | solution.py:167
  270.9 5.0 %all-to-all-start.3 = ((bf16[16,8,4096]{2,1,0:T(8,128)(2,1)}), bf16[16,8,4096]{2,1,0:T(8,128)(2,1)S(1)}, u32[]{:S(2)}, u32[]{:S(2)}) async-start(bf16[16,8,4096]{2,1,0:T(8,128)(2,1)} %fusion.10), calls=%async_computation.4 | async-start | bytes 2097152 | tf_op jit(solution)/shard_map/all_to_all | solution.py:168
  276.1 22.7 %all-to-all-done.3 = bf16[16,8,4096]{2,1,0:T(8,128)(2,1)S(1)} async-done(((bf16[16,8,4096]{2,1,0:T(8,128)(2,1)}), bf16[16,8,4096]{2,1,0:T(8,128)(2,1)S(1)}, u32[]{:S(2)}, u32[]{:S(2)}) %all-to-all-start.3) | async-done | bytes 1048608 | tf_op jit(solution)/shard_map/all_to_all | solution.py:168
  298.8 2.1 fusion.13
  (67 shorter events, 16.9 us)
Async XLA Ops:
  6.5 151.4 %copy-start = (bf16[256,4096]{1,0:T(8,128)(2,1)S(1)}, bf16[256,4096]{1,0:T(8,128)(2,1)}, u32[]{:S(2)}) copy-start(bf16[256,4096]{1,0:T(8,128)(2,1)} %param.23) | copy-start | bytes 6291460
  6.5 47.1 %all-gather.2.cloned.1.call-start = ((), (), s32[]{:S(2)}) async-start(), calls=%async_computation.5 | async-start | bytes 2228224 | tf_op jit(solution)/shard_map/all_gather | solution.py:99
  71.9 7.0 %copy-start.2 = (f32[128,32]{1,0:T(8,128)S(1)}, f32[128,32]{1,0:T(8,128)}, u32[]{:S(2)}) copy-start(f32[128,32]{1,0:T(8,128)} %copy.127) | copy-start | bytes 49156
  73.5 35.8 %all-to-all-start = ((f32[1,256,32]{1,0,2:T(1,128)}), f32[1,256,32]{1,0,2:T(1,128)S(1)}, u32[]{:S(2)}, u32[]{:S(2)}) async-start(f32[1,256,32]{1,0,2:T(1,128)} %copy.124), calls=%async_computation | async-start | bytes 65536 | tf_op jit(solution)/shard_map/all_to_all | solution.py:116
  78.9 4.5 %copy-start.8 = (s32[128]{0:T(128)S(1)}, s32[128]{0:T(128)}, u32[]{:S(2)}) copy-start(s32[128]{0:T(128)} %param.19) | copy-start | bytes 1540
  83.4 19.0 %copy-start.3 = (f32[16,32]{1,0:T(8,128)S(1)}, f32[16,32]{1,0:T(8,128)}, u32[]{:S(2)}) copy-start(f32[16,32]{1,0:T(8,128)} %get-tuple-element.8) | copy-start | bytes 6148
  83.4 19.0 %copy-start.4 = (f32[16,32]{1,0:T(8,128)S(1)}, f32[16,32]{1,0:T(8,128)}, u32[]{:S(2)}) copy-start(f32[16,32]{1,0:T(8,128)} %get-tuple-element.9) | copy-start | bytes 6148
  109.3 45.8 %all-to-all-start.1 = ((bf16[1,256,32,128]{3,1,0,2:T(8,128)(2,1)}), bf16[1,256,32,128]{3,1,0,2:T(8,128)(2,1)}, u32[]{:S(2)}, u32[]{:S(2)}) async-start(bf16[1,256,32,128]{3,1,0,2:T(8,128)(2,1)} %copy.128), calls=%async_computation.1 | async-start | bytes 4194304 | tf_op jit(solution)/shard_map/all_to_all | solution.py:117
  113.9 114.3 %reduce-scatter.2.cloned.1.call-start = ((), (), s32[]{:S(2)}) async-start(), calls=%async_computation.6 | async-start | bytes 2228224 | tf_op jit(solution)/shard_map/reduce_scatter | solution.py:127
  155.1 4.9 %copy-start.7 = (s32[16,8]{0,1:T(8,128)S(1)}, s32[16,8]{0,1:T(8,128)}, u32[]{:S(2)}) copy-start(s32[16,8]{0,1:T(8,128)} %param.21) | copy-start | bytes 1540
  157.6 3.1 %copy-start.6 = (bf16[4096]{0:T(1024)(128)(2,1)S(1)}, bf16[4096]{0:T(1024)(128)(2,1)}, u32[]{:S(2)}) copy-start(bf16[4096]{0:T(1024)(128)(2,1)} %param.24) | copy-start | bytes 24580
  157.6 70.6 %copy-start.1 = (bf16[16,4096]{1,0:T(8,128)(2,1)S(1)}, bf16[16,4096]{1,0:T(8,128)(2,1)}, u32[]{:S(2)}) copy-start(bf16[16,4096]{1,0:T(8,128)(2,1)} %param.14) | copy-start | bytes 393220
  262.8 13.1 %copy-start.5 = (s32[16,8]{0,1:T(8,128)S(1)}, s32[16,8]{0,1:T(8,128)}, u32[]{:S(2)}) copy-start(s32[16,8]{0,1:T(8,128)} %param.22) | copy-start | bytes 1540
  270.9 27.9 %all-to-all-start.3 = ((bf16[16,8,4096]{2,1,0:T(8,128)(2,1)}), bf16[16,8,4096]{2,1,0:T(8,128)(2,1)S(1)}, u32[]{:S(2)}, u32[]{:S(2)}) async-start(bf16[16,8,4096]{2,1,0:T(8,128)(2,1)} %fusion.10), calls=%async_computation.4 | async-start | bytes 2097152 | tf_op jit(solution)/shard_map/all_to_all | solution.py:168
Sparse Core Ops, SparseCore 0:
  9.5 44.0 all-gather.1
  160.1 68.0 reduce-scatter.1
where the time goes:
time: 310 us; the launch traced here: 308 us
  waiting for transfers between devices  174 us (56%)
  other arithmetic  38.8 us (13%)
  blocking collectives  28.3 us (9%)
  matrix products  22.7 us (7%)
  local copies, waits for them, and re-layouts  16.9 us (5%)
  between operations  13.7 us (4%)
  starting transfers between devices  13.4 us (4%)
    reduce_scatter x1, waiting for transfers between devices, on_device(): lax.psum_scatter(jnp.dot(attn_local, out_proj, preferred_element_type=jnp...  67.4 us
    all_gather x1, waiting for transfers between devices, on_device(): query_all = lax.all_gather(queries, 'dev', axis=0, tiled=True)  42.3 us
    all_to_all x1, waiting for transfers between devices, on_device(): lax.all_to_all(table_share[None], 'dev', split_axis=2, concat_axis=0, til...  40.8 us
    all_to_all x1, blocking collectives, on_device(): lax.all_to_all(outgoing, 'dev', split_axis=0, concat_axis=0, tiled=True)  28.3 us
    all_to_all x1, waiting for transfers between devices, on_device(): lax.all_to_all(result.reshape(sources, slot_count, result.shape[1]), 'dev...  22.7 us
    scatter-add x1, other arithmetic, reduce_rows(): jax.ops.segment_sum(seg_out * weight[..., None], row_ids, num_segments=ro...  19 us
    dot_general x1, matrix products, on_device(): jnp.dot(activated, w_down[0], preferred_element_type=jnp.float32)  8.06 us
  transfers between devices with their start and end apart: 5, of which 4 were waited for; matrix products, arithmetic and copies ran while one was open for 12% of the time, Pallas kernels for 0%

commit v1 on v0

v1 whole, which is shorter than its diff:
```python
import functools

import jax
import jax.numpy as jnp
from jax import lax
from jax.experimental import pallas as pl
from jax.experimental.pallas import tpu as pltpu
from jax.sharding import PartitionSpec as P

HEAD_SIZE = 128
HQ = 32
LANES = 128
BLOCK_SEGS = 16
LOW = -1e30
F32 = jnp.float32
BF16 = jnp.bfloat16


def halves(width):
    if width % (2 * LANES) == 0:
        return [(0, width // 2), (width // 2, width // 2)]
    return [(0, width)]


def bit_orders(levels):
    first = list(range(levels))
    second = list(first)
    if levels >= 4:
        second[1], second[2] = second[2], second[1]
    return [first, second]


def layer_kernel(
    dims,
    hidden_ref,
    query_ref,
    fresh_ref,
    key_hbm,
    value_hbm,
    owner_ref,
    bias_ref,
    gates_ref,
    proj_hbm,
    gain_ref,
    wg_hbm,
    wu_hbm,
    wd_hbm,
    out_ref,
    key_v,
    value_v,
    proj_v,
    wg_v,
    wu_v,
    wd_v,
    load_sem,
    gathered,
    gate_all,
    seg_query,
    seg_out,
    table,
    table_in,
    lse_tab,
    lse_in,
    part,
    part_in,
    normed_all,
    act_v,
    send_sem,
    recv_sem,
):
    n, levels, row_dev, model, ff, segs, slots, kv_heads, per_dev, pos, pos_lanes = dims
    rows = n * row_dev
    group_size = HQ // kv_heads
    hd = HQ * HEAD_SIZE
    own_cols = per_dev * HEAD_SIZE
    me = lax.axis_index("dev")
    orders = bit_orders(levels)

    def my_bit(k):
        return lax.rem(lax.div(me, 2**k), 2)

    def partner(k):
        return me + (1 - 2 * my_bit(k)) * 2**k

    def axis_of(k):
        return levels - 1 - k

    def static_index(d):
        return tuple((d // 2**k) % 2 for k in reversed(range(levels)))

    mine = tuple(my_bit(k) for k in reversed(range(levels)))

    loads = []
    for i, (src, dst) in enumerate(
        [
            (key_hbm, key_v),
            (value_hbm, value_v),
            (proj_hbm, proj_v),
            (wg_hbm.at[0], wg_v),
            (wu_hbm.at[0], wu_v),
            (wd_hbm.at[0], wd_v),
        ]
    ):
        copy = pltpu.make_async_copy(src, dst, load_sem.at[i])
        copy.start()
        loads.append(copy)

    barrier = pltpu.get_barrier_semaphore()
    for k in range(levels):
        pl.semaphore_signal(
            barrier, inc=1, device_id={"dev": partner(k)}, device_id_type=pl.DeviceIdType.MESH
        )
    pl.semaphore_wait(barrier, levels)

    def remote(src, dst, phase, piece, step, bit):
        copy = pltpu.make_async_remote_copy(
            src_ref=src,
            dst_ref=dst,
            send_sem=send_sem.at[phase, piece, step],
            recv_sem=recv_sem.at[phase, piece, step],
            device_id={"dev": partner(bit)},
            device_id_type=pl.DeviceIdType.MESH,
        )
        copy.start()
        return copy

    def gather(pieces):
        copies = []
        pending = [None] * len(pieces)
        for step in range(levels):
            for i, (buf, c0, width, order, phase, piece) in enumerate(pieces):
                down = order[::-1]
                if pending[i] is not None:
                    pending[i].wait_recv()
                index = [slice(None)] * levels
                for k in down[step:]:
                    index[axis_of(k)] = my_bit(k)
                ref = buf.at[tuple(index) + (slice(None), pl.ds(c0, width))]
                pending[i] = remote(ref, ref, phase, piece, step, down[step])
                copies.append(pending[i])
        for copy in pending:
            copy.wait_recv()
        for copy in copies:
            copy.wait_send()

    def scatter_sum(pieces):
        copies = []
        pending = [None] * len(pieces)

        def offset_of(step):
            return sum(n >> (t + 1) for t in range(step))

        def add(i, step):
            buf, arrivals, c0, width, order, phase, piece = pieces[i]
            count = n >> (step + 1)
            free = [k for k in reversed(range(levels)) if k not in order[: step + 1]]

            def body(j, carry):
                index = list(mine)
                for place, k in enumerate(reversed(free)):
                    index[axis_of(k)] = lax.rem(lax.div(j, 2**place), 2)
                index = tuple(index) + (slice(None), pl.ds(c0, width))
                buf[index] = buf[index] + arrivals[offset_of(step) + j, :, pl.ds(c0, width)]
                return carry

            lax.fori_loop(0, count, body, 0)

        for step in range(levels):
            for i, (buf, arrivals, c0, width, order, phase, piece) in enumerate(pieces):
                if step > 0:
                    pending[i].wait_recv()
                    add(i, step - 1)
                bit = order[step]
                free = [k for k in reversed(range(levels)) if k not in order[: step + 1]]
                count = n >> (step + 1)
                copy = None
                for j in range(count):
                    index = [None] * levels
                    for k in order[:step]:
                        index[axis_of(k)] = my_bit(k)
                    index[axis_of(bit)] = 1 - my_bit(bit)
                    for place, k in enumerate(reversed(free)):
                        index[axis_of(k)] = (j // 2**place) % 2
                    cols = pl.ds(c0, width)
                    copy = pltpu.make_async_remote_copy(
                        src_ref=buf.at[tuple(index) + (slice(None), cols)],
                        dst_ref=arrivals.at[offset_of(step) + j, :, cols],
                        send_sem=send_sem.at[phase, piece, step],
                        recv_sem=recv_sem.at[phase, piece, step],
                        device_id={"dev": partner(bit)},
                        device_id_type=pl.DeviceIdType.MESH,
                    )
                    copy.start()
                span = arrivals.at[pl.ds(offset_of(step), count), :, pl.ds(c0, width)]
                whole = pltpu.make_async_remote_copy(
                    src_ref=span,
                    dst_ref=span,
                    send_sem=send_sem.at[phase, piece, step],
                    recv_sem=recv_sem.at[phase, piece, step],
                    device_id={"dev": partner(bit)},
                    device_id_type=pl.DeviceIdType.MESH,
                )
                pending[i] = whole
                copies.append(whole)
        for i in range(len(pieces)):
            pending[i].wait_recv()
            add(i, levels - 1)
        for copy in copies:
            copy.wait_send()

    gathered[mine + (slice(None), pl.ds(0, hd))] = query_ref[...]
    gathered[mine + (slice(None), pl.ds(hd, fresh_ref.shape[1]))] = fresh_ref[...]
    gate_all[mine] = gates_ref[...]
    pieces = [(gate_all, 0, LANES, orders[0], 1, 0)]
    for i, (c0, width) in enumerate(halves(gathered.shape[-1])):
        pieces.append((gathered, c0, width, orders[i], 0, i))
    gather(pieces)

    owner = owner_ref[...]
    owner_col = owner[:, :1]
    pick = (lax.broadcasted_iota(jnp.int32, (segs, rows), 1) == owner_col).astype(BF16)
    tile = 512

    def pick_queries(j, carry):
        cols = pl.ds(pl.multiple_of(j * tile, tile), tile)
        block = gathered[(slice(None),) * levels + (slice(None), cols)].reshape(rows, tile)
        seg_query[:, cols] = jnp.dot(pick, block, preferred_element_type=F32).astype(BF16)
        return carry

    lax.fori_loop(0, hd // tile, pick_queries, 0)
    loads[0].wait()
    loads[1].wait()

    wide = BLOCK_SEGS * slots
    tall = BLOCK_SEGS * group_size
    row_seg = lax.rem(lax.broadcasted_iota(jnp.int32, (tall, wide), 0), BLOCK_SEGS)
    col_seg = lax.div(lax.broadcasted_iota(jnp.int32, (tall, wide), 1), slots)
    same = row_seg == col_seg
    lane_of = lax.broadcasted_iota(jnp.int32, (BLOCK_SEGS, LANES), 1)
    scale = HEAD_SIZE ** (-0.5)
    stat_max = []
    stat_sum = []
    for b in range(segs // BLOCK_SEGS):
        span = pl.ds(b * BLOCK_SEGS, BLOCK_SEGS)
        bias = bias_ref[b]
        block_max = jnp.zeros((BLOCK_SEGS, LANES), F32)
        block_sum = jnp.zeros((BLOCK_SEGS, LANES), F32)
        for g in range(kv_heads):
            kcols = pl.ds(g * HEAD_SIZE, HEAD_SIZE)
            keys = key_v[span, :, kcols].reshape(wide, HEAD_SIZE)
            values = value_v[span, :, kcols].reshape(wide, HEAD_SIZE)
            stacked = jnp.concatenate(
                [
                    seg_query[span, pl.ds((g * group_size + h) * HEAD_SIZE, HEAD_SIZE)]
                    for h in range(group_size)
                ],
                axis=0,
            )
            scores = lax.dot_general(
                stacked, keys, (((1,), (1,)), ((), ())), preferred_element_type=F32
            )
            scores = jnp.where(same, scores * scale + bias, LOW)
            top = jnp.max(scores, axis=1, keepdims=True)
            prob = jnp.exp(scores - top)
            total = jnp.sum(prob, axis=1, keepdims=True)
            out = jnp.dot(prob.astype(BF16), values, preferred_element_type=F32)
            for h in range(group_size):
                head = g * group_size + h
                lines = slice(h * BLOCK_SEGS, (h + 1) * BLOCK_SEGS)
                seg_out[span, pl.ds(head * HEAD_SIZE, HEAD_SIZE)] = out[lines]
                block_max = jnp.where(lane_of == head, top[lines], block_max)
                block_sum = jnp.where(lane_of == head, total[lines], block_sum)
        stat_max.append(block_max)
        stat_sum.append(block_sum)
    seg_max = jnp.concatenate(stat_max, axis=0)
    seg_sum = jnp.concatenate(stat_sum, axis=0)

    place = lax.broadcasted_iota(jnp.int32, (segs, LANES), 0)

    def scan(value, combine, forward):
        sh = 1
        while sh < segs:
            amount = sh if forward else segs - sh
            moved = pltpu.roll(value, amount, 0)
            near = pltpu.roll(owner, amount, 0)
            inside = (place >= sh) if forward else (place < segs - sh)
            value = jnp.where(inside & (near == owner), combine(value, moved), value)
            sh *= 2
        return value

    row_max = scan(scan(seg_max, jnp.maximum, True), jnp.maximum, False)
    weight = jnp.exp(seg_max - row_max)
    row_sum = scan(seg_sum * weight, jnp.add, True)
    row_sum = jnp.maximum(scan(row_sum, jnp.maximum, False), 1.0)
    row_lse = row_max + jnp.log(row_sum)
    weight = weight / row_sum
    first = (place == 0) | (pltpu.roll(owner, 1, 0) != owner)
    lane = lax.broadcasted_iota(jnp.int32, (segs, LANES), 1)
    stats = jnp.where(lane == HQ, (owner + 1).astype(F32), row_lse)
    stats = jnp.where(first & (lane <= HQ), stats, 0.0)

    to_place = (lax.broadcasted_iota(jnp.int32, (segs, pos_lanes), 1) == owner_col + me).astype(F32)
    stats_t = jnp.dot(
        stats.T, to_place, precision=lax.Precision.HIGHEST, preferred_element_type=F32
    )
    spare = jnp.zeros((8 - per_dev - 1, pos_lanes), F32)
    for d in range(n):
        lse_tab[static_index(d)] = jnp.concatenate(
            [stats_t[d * per_dev : (d + 1) * per_dev], stats_t[HQ : HQ + 1], spare], axis=0
        )
    put = (
        lax.broadcasted_iota(jnp.int32, (pos, segs), 0) == owner_ref[:, :].T[:1, :] + me
    ).astype(BF16)
    for d in range(n):
        scaled = jnp.concatenate(
            [
                (
                    seg_out[:, pl.ds(head * HEAD_SIZE, HEAD_SIZE)] * weight[:, head : head + 1]
                ).astype(BF16)
                for head in range(d * per_dev, (d + 1) * per_dev)
            ],
            axis=1,
        )
        table[static_index(d)] = jnp.dot(put, scaled, preferred_element_type=F32).astype(BF16)

    pieces = [(lse_tab, lse_in, 0, pos_lanes, orders[0], 3, 0)]
    for i, (c0, width) in enumerate(halves(own_cols)):
        pieces.append((table, table_in, c0, width, orders[i], 2, i))
    scatter_sum(pieces)

    my_lse = lse_tab[mine]
    my_table = table[mine]
    row_of = my_lse[per_dev : per_dev + 1, :].astype(jnp.int32) - 1
    hit = lax.broadcasted_iota(jnp.int32, (rows, pos_lanes), 0) == row_of
    heads = []
    full = (slice(None),) * (levels + 1)
    for h in range(per_dev):
        head = me * per_dev + h
        g = lax.div(head, group_size)
        q_cols = pl.ds(pl.multiple_of(head * HEAD_SIZE, HEAD_SIZE), HEAD_SIZE)
        k_cols = pl.ds(pl.multiple_of(hd + g * HEAD_SIZE, HEAD_SIZE), HEAD_SIZE)
        v_cols = pl.ds(pl.multiple_of(hd + (kv_heads + g) * HEAD_SIZE, HEAD_SIZE), HEAD_SIZE)
        q = gathered[full + (q_cols,)].reshape(rows, HEAD_SIZE).astype(F32)
        k = gathered[full + (k_cols,)].reshape(rows, HEAD_SIZE).astype(F32)
        v = gathered[full + (v_cols,)].reshape(rows, HEAD_SIZE).astype(F32)
        own = jnp.sum(q * k, axis=1, keepdims=True) * scale
        lse = jnp.where(hit, my_lse[h : h + 1, :], LOW)
        top = jnp.maximum(jnp.max(lse, axis=1, keepdims=True), own)
        share = jnp.exp(lse - top)
        fresh = jnp.exp(own - top)
        inverse = 1.0 / (jnp.sum(share, axis=1, keepdims=True) + fresh)
        mixed_in = jnp.dot(
            (share * inverse)[:, :pos].astype(BF16),
            my_table[:, h * HEAD_SIZE : (h + 1) * HEAD_SIZE],
            preferred_element_type=F32,
        )
        heads.append((mixed_in + v * (fresh * inverse)).astype(BF16))
    attention = jnp.concatenate(heads, axis=1) if per_dev > 1 else heads[0]

    loads[2].wait()

    def project(j, carry):
        cols = pl.ds(pl.multiple_of(j * tile, tile), tile)
        product = jnp.dot(attention, proj_v[:, cols], preferred_element_type=F32)
        part[full + (cols,)] = product.astype(BF16).reshape((2,) * levels + (row_dev, tile))
        return carry

    lax.fori_loop(0, model // tile, project, 0)
    scatter_sum(
        [
            (part, part_in, c0, width, orders[i], 4, i)
            for i, (c0, width) in enumerate(halves(model))
        ]
    )

    mixed = (hidden_ref[...].astype(F32) + part[mine].astype(F32)).astype(BF16).astype(F32)
    scale_row = lax.rsqrt(jnp.mean(mixed * mixed, axis=1, keepdims=True) + 1e-06)
    normed_all[mine] = (mixed * scale_row * gain_ref[...].astype(F32)).astype(BF16)
    gather(
        [(normed_all, c0, width, orders[i], 5, i) for i, (c0, width) in enumerate(halves(model))]
    )

    all_gates = gate_all[...].reshape(rows, LANES)
    gate_lane = lax.broadcasted_iota(jnp.int32, (rows, LANES), 1)
    gate = jnp.sum(jnp.where(gate_lane == me, all_gates, 0.0), axis=1, keepdims=True)
    loads[3].wait()
    loads[4].wait()
    ff_tile = 256

    def hidden_units(j, carry):
        cols = pl.ds(pl.multiple_of(j * ff_tile, ff_tile), ff_tile)
        tokens = normed_all[...].reshape(rows, model)
        gate_proj = jnp.dot(tokens, wg_v[:, cols], preferred_element_type=F32)
        up_proj = jnp.dot(tokens, wu_v[:, cols], preferred_element_type=F32)
        act_v[:, cols] = (jax.nn.silu(gate_proj) * up_proj).astype(BF16)
        return carry

    lax.fori_loop(0, ff // ff_tile, hidden_units, 0)
    loads[5].wait()

    def down(j, carry):
        cols = pl.ds(pl.multiple_of(j * tile, tile), tile)
        product = jnp.dot(act_v[...], wd_v[:, cols], preferred_element_type=F32)
        part[full + (cols,)] = (
            (product * gate).astype(BF16).reshape((2,) * levels + (row_dev, tile))
        )
        return carry

    lax.fori_loop(0, model // tile, down, 0)
    scatter_sum(
        [
            (part, part_in, c0, width, orders[i], 6, i)
            for i, (c0, width) in enumerate(halves(model))
        ]
    )
    out_ref[...] = (mixed + part[mine].astype(F32)).astype(BF16)


def on_device(
    hidden_in,
    queries,
    fresh_key_value,
    segment_key_cache,
    segment_value_cache,
    segment_owner_row,
    segment_length,
    expert_ids,
    gate_score,
    out_proj,
    norm_gain,
    w_gate,
    w_up,
    w_down,
):
    n = lax.axis_size("dev")
    levels = n.bit_length() - 1
    row_dev, model = hidden_in.shape
    segs, slots, kv_width = segment_key_cache.shape
    kv_heads = kv_width // HEAD_SIZE
    ff = w_gate.shape[2]
    per_dev = HQ // n
    rows = n * row_dev
    pos = rows + n
    pos_lanes = -(-pos // LANES) * LANES
    dims = (n, levels, row_dev, model, ff, segs, slots, kv_heads, per_dev, pos, pos_lanes)
    own_cols = per_dev * HEAD_SIZE
    hd = queries.shape[1]
    fresh = fresh_key_value.reshape(row_dev, 2 * kv_width)
    owner = jnp.broadcast_to(segment_owner_row[:, None], (segs, LANES))
    live = jnp.arange(slots, dtype=jnp.int32)[None, :] < segment_length[:, None]
    bias = jnp.where(live, 0.0, LOW).astype(F32).reshape(
        segs // BLOCK_SEGS, 1, BLOCK_SEGS * slots
    )
    probs = jnp.exp(gate_score.astype(F32) / 4.0)
    probs = probs / jnp.sum(probs, axis=1, keepdims=True)
    chosen = expert_ids[:, :, None] == jnp.arange(LANES, dtype=jnp.int32)[None, None, :]
    gates = jnp.sum(jnp.where(chosen, probs[:, :, None], 0.0), axis=1)
    cube = (2,) * levels
    vmem = pl.BlockSpec(memory_space=pltpu.VMEM)
    hbm = pl.BlockSpec(memory_space=pl.ANY)
    return pl.pallas_call(
        functools.partial(layer_kernel, dims),
        out_shape=jax.ShapeDtypeStruct((row_dev, model), BF16),
        in_specs=[vmem, vmem, vmem, hbm, hbm, vmem, vmem, vmem, hbm, vmem, hbm, hbm, hbm],
        out_specs=vmem,
        scratch_shapes=[
            pltpu.VMEM(segment_key_cache.shape, BF16),
            pltpu.VMEM(segment_value_cache.shape, BF16),
            pltpu.VMEM(out_proj.shape, BF16),
            pltpu.VMEM(w_gate.shape[1:], BF16),
            pltpu.VMEM(w_up.shape[1:], BF16),
            pltpu.VMEM(w_down.shape[1:], BF16),
            pltpu.SemaphoreType.DMA((6,)),
            pltpu.VMEM(cube + (row_dev, hd + 2 * kv_width), BF16),
            pltpu.VMEM(cube + (row_dev, LANES), F32),
            pltpu.VMEM((segs, hd), BF16),
            pltpu.VMEM((segs, hd), F32),
            pltpu.VMEM(cube + (pos, own_cols), BF16),
            pltpu.VMEM((n - 1, pos, own_cols), BF16),
            pltpu.VMEM(cube + (8, pos_lanes), F32),
            pltpu.VMEM((n - 1, 8, pos_lanes), F32),
            pltpu.VMEM(cube + (row_dev, model), BF16),
            pltpu.VMEM((n - 1, row_dev, model), BF16),
            pltpu.VMEM(cube + (row_dev, model), BF16),
            pltpu.VMEM((rows, ff), BF16),
            pltpu.SemaphoreType.DMA((7, 2, levels)),
            pltpu.SemaphoreType.DMA((7, 2, levels)),
        ],
        compiler_params=pltpu.CompilerParams(
            collective_id=0, has_side_effects=True, vmem_limit_bytes=60 * 2**20
        ),
        name="decode_layer",
    )(
        hidden_in,
        queries,
        fresh,
        segment_key_cache,
        segment_value_cache,
        owner,
        bias,
        gates,
        out_proj,
        norm_gain.reshape(1, model),
        w_gate,
        w_up,
        w_down,
    )


def solution(mesh):
    placed = (
        P(("groups", "dev"), None),
        P(("groups", "dev"), None),
        P(("groups", "dev"), None, None),
        P(("groups", "dev"), None, None),
        P(("groups", "dev"), None, None),
        P(("groups", "dev")),
        P(("groups", "dev")),
        P(("groups", "dev"), None),
        P(("groups", "dev"), None),
        P("dev", None),
        P(),
        P("dev", None, None),
        P("dev", None, None),
        P("dev", None, None),
    )
    return jax.shard_map(
        on_device, mesh=mesh, in_specs=placed, out_specs=P(("groups", "dev"), None), check_vma=False
    )
```

time: 310 us -> 138 us (0.45)
  waiting for transfers between devices: 174 us -> 0 us
  Pallas kernels: 0 us -> 127 us
  other arithmetic: 38.8 us -> 2.71 us
  blocking collectives: 28.3 us -> 0 us
  matrix products: 22.7 us -> 0 us
  between operations: 13.7 us -> 0.02 us
  starting transfers between devices: 13.4 us -> 0 us
  local copies, waits for them, and re-layouts: 16.9 us -> 7.38 us
    pallas_call x0 -> x1, Pallas kernels: none -> 127 us  [on_device(): pl.pallas_call(functools.partial(layer_kernel, dims), out_shape=jax.Shape...]
    reduce_scatter x1 -> x0, waiting for transfers between devices: 67.4 us -> none  [on_device(): lax.psum_scatter(jnp.dot(attn_local, out_proj, preferred_element_type=jnp...]
    all_to_all x3 -> x0, waiting for transfers between devices: 63.5 us -> none  [the longest x1 40.8 us: on_device(): lax.all_to_all(table_share[None], 'dev', split_axis=2, concat_axis=0, til...]
    all_gather x1 -> x0, waiting for transfers between devices: 42.3 us -> none  [on_device(): query_all = lax.all_gather(queries, 'dev', axis=0, tiled=True)]
    all_to_all x1 -> x0, blocking collectives: 28.3 us -> none  [on_device(): lax.all_to_all(outgoing, 'dev', split_axis=0, concat_axis=0, tiled=True)]
    dot_general x7 -> x0, matrix products: 22.7 us -> none  [the longest x1 8.06 us: on_device(): jnp.dot(activated, w_down[0], preferred_element_type=jnp.float32)]
    scatter-add x2 -> x0, other arithmetic: 20.6 us -> none  [the longest x1 19 us: reduce_rows(): jax.ops.segment_sum(seg_out * weight[..., None], row_ids, num_segments=ro...]
    all_to_all x3 -> x0, starting transfers between devices: 13.1 us -> none  [the longest x1 4.99 us: on_device(): lax.all_to_all(result.reshape(sources, slot_count, result.shape[1]), 'dev...]
  transfers between devices with their start and end apart: 5 -> 0, of which waited for: 4 -> 0; matrix products, arithmetic and copies ran while one was open for 12% -> 0% of each run, Pallas kernels for 0% -> 0%
where the time goes in v1:
time: 138 us; the launch traced here: 137 us
  Pallas kernels  127 us (92%)
  local copies, waits for them, and re-layouts  7.38 us (5%)
  other arithmetic  2.71 us (2%)
    pallas_call x1, Pallas kernels, on_device(): pl.pallas_call(functools.partial(layer_kernel, dims), out_shape=jax.Shape...  127 us
    unnamed x3, local copies, waits for them, and re-layouts  3.65 us

profile of v1, /device:TPU:0, one launch (start us, length us, event | category | flops | bytes accessed | tf_op | source)
XLA Modules:
  0.0 137.2 jit_solution(6366058581470260061)
XLA Ops:
  0.0 0.7 fusion.1
  0.7 0.7 fusion
  1.4 0.1 copy.18
  1.5 0.7 lt.31
  2.2 0.8 copy.17
  3.0 0.7 select_reduce_fusion.gates_ref
  3.7 0.1 lt.29
  3.8 1.3 copy.19
  5.1 1.3 reshape.55.gain_ref
  6.4 0.1 lt.32
  6.5 0.1 lt.33
  6.6 0.6 compare_select_fusion.bias_ref
  7.2 1.4 broadcast_in_dim.32.owner_ref
  8.5 127.1 %decode_layer.1 = bf16[16,4096]{1,0:T(8,128)(2,1)} custom-call(bf16[16,4096]{1,0:T(8,128)(2,1)} %hidden_ref.1, bf16[16,4096]{1,0:T(8,128)(2,1)} %query_ref.1, bf16[16,512]{1,0:T(8,128)(2,1)} %bitcast.2, bf16[128,16,256]{2,1,0:T(8,128)(2,1)} %key_hbm.1, bf16[128,16,256]{2,1,0:T(8,128)(2,1)} %value_hbm.1, s32[128,128]{1,0:T(8,128)} %broadcast_in_dim.32.owner_ref, ...), custom_call_target="tpu_custom_call" | custom-call | tf_op jit(solution)/shard_map/decode_layer/pallas_call | solution.py:461
  135.6 1.6 %copy.21 = bf16[16,4096]{1,0:T(8,128)(2,1)} copy(bf16[16,4096]{1,0:T(8,128)(2,1)} %decode_layer.1) | data formatting | bytes 262144
  (1 shorter events, 0.0 us)

commit v2 on v1

v2 whole, which is shorter than its diff:
```python
import functools

import jax
import jax.numpy as jnp
from jax import lax
from jax.experimental import pallas as pl
from jax.experimental.pallas import tpu as pltpu
from jax.sharding import PartitionSpec as P

HEAD_SIZE = 128
HQ = 32
LANES = 128
BLOCK_SEGS = 16
LOW = -1e30
F32 = jnp.float32
BF16 = jnp.bfloat16


def halves(width, unit):
    half = width // unit // 2 * unit
    return [(0, half), (half, width - half)]


def layer_kernel(
    dims,
    hidden_hbm,
    query_hbm,
    fresh_ref,
    key_hbm,
    value_hbm,
    owner_ref,
    length_ref,
    ids_ref,
    score_ref,
    proj_hbm,
    gain_ref,
    wg_hbm,
    wu_hbm,
    wd_hbm,
    out_ref,
    key_v,
    value_v,
    proj_v,
    wg_v,
    wu_v,
    wd_v,
    hidden_v,
    load_sem,
    gathered,
    gate_all,
    seg_query,
    seg_out,
    table,
    table_sib,
    table_ring,
    lse_tab,
    lse_sib,
    lse_ring,
    part,
    part_sib,
    part_ring,
    normed_all,
    act_v,
    send_sem,
    recv_sem,
):
    n, snake, row_dev, model, ff, segs, slots, kv_heads, per_dev, pos, pos_lanes = dims
    rows = n * row_dev
    group_size = HQ // kv_heads
    hd = HQ * HEAD_SIZE
    kv_width = kv_heads * HEAD_SIZE
    own_cols = per_dev * HEAD_SIZE
    me = lax.axis_index("dev")

    chips = n // 2
    reach = chips // 2
    core = lax.rem(me, 2)
    chip = lax.div(me, 2)
    if snake:
        side = lax.rem(chip, 2)
        along = lax.div(chip, 2)
        spot = along * (1 - side) + (chips - 1 - along) * side
    else:
        spot = chip

    def chip_at(offset):
        p = lax.rem(spot + offset + chips, chips)
        if not snake:
            return p
        back = lax.div(p, chips // 2)
        return (1 - back) * 2 * p + back * (2 * (chips - 1 - p) + 1)

    sibling = chip * 2 + 1 - core
    beside = {d: chip_at(d) * 2 + core for d in (1, -1)}
    offsets = [reach]
    for dist in range(reach - 1, 0, -1):
        offsets += [dist, -dist]
    offsets.append(0)

    def slot_of(offset):
        return offsets.index(reach if offset == -reach else offset)

    def ring_slot(d, step):
        return chips + (0 if d == 1 else reach) + step

    loads = []
    for i, (src, dst) in enumerate(
        [
            (query_hbm, gathered.at[me, :, pl.ds(0, hd)]),
            (key_hbm, key_v),
            (value_hbm, value_v),
            (hidden_hbm, hidden_v),
            (proj_hbm, proj_v),
            (wg_hbm.at[0], wg_v),
            (wu_hbm.at[0], wu_v),
            (wd_hbm.at[0], wd_v),
        ]
    ):
        copy = pltpu.make_async_copy(src, dst, load_sem.at[i])
        copy.start()
        loads.append(copy)

    barrier = pltpu.get_barrier_semaphore()
    for other in (beside[1], beside[-1], sibling):
        pl.semaphore_signal(
            barrier, inc=1, device_id={"dev": other}, device_id_type=pl.DeviceIdType.MESH
        )

    def remote(src, dst, phase, piece, slot, device):
        copy = pltpu.make_async_remote_copy(
            src_ref=src,
            dst_ref=dst,
            send_sem=send_sem.at[phase, piece, slot],
            recv_sem=recv_sem.at[phase, piece, slot],
            device_id={"dev": device},
            device_id_type=pl.DeviceIdType.MESH,
        )
        copy.start()
        return copy

    def gather(phase, pieces):
        copies = []
        ring = {}
        beside_me = []

        def to_sibling(i, offset):
            buf, cut, far = pieces[i]
            ref = buf.at[(chip_at(offset) * 2 + core,) + cut]
            copy = remote(ref, ref, phase, i, slot_of(offset), sibling)
            copies.append(copy)
            beside_me.append(copy)

        for step in range(reach):
            for i, (buf, cut, far) in enumerate(pieces):
                for d in (1, -1):
                    if step > 0:
                        ring[d, step - 1, i].wait_recv()
                    if step == reach - 1 and far != d:
                        continue
                    ref = buf.at[(chip_at(-d * step) * 2 + core,) + cut]
                    copy = remote(ref, ref, phase, i, ring_slot(d, step), beside[d])
                    ring[d, step, i] = copy
                    copies.append(copy)
            for i in range(len(pieces)):
                for offset in (step, -step) if step else (0,):
                    to_sibling(i, offset)
        for i, (buf, cut, far) in enumerate(pieces):
            ring[far, reach - 1, i].wait_recv()
            to_sibling(i, reach)
        for copy in beside_me:
            copy.wait_recv()
        for copy in copies:
            copy.wait_send()

    def scatter_sum(phase, pieces):
        copies = []
        ring = {}
        near = {}
        for offset in offsets:
            for i, (buf, sib, ring_in, cut, far) in enumerate(pieces):
                slot = slot_of(offset)
                copy = remote(
                    buf.at[(chip_at(offset) * 2 + 1 - core,) + cut],
                    sib.at[(slot,) + cut],
                    phase,
                    i,
                    slot,
                    sibling,
                )
                copies.append(copy)
                near[slot, i] = copy
        for step in range(reach):
            for i, (buf, sib, ring_in, cut, far) in enumerate(pieces):
                for d in (1, -1):
                    if step == 0 and far != d:
                        continue
                    offset = d * (reach - step)
                    slot = slot_of(offset)
                    where = (chip_at(offset) * 2 + core,) + cut
                    near[slot, i].wait_recv()
                    total = buf[where].astype(F32) + sib[(slot,) + cut].astype(F32)
                    if (d, step - 1, i) in ring:
                        ring[d, step - 1, i].wait_recv()
                        total = total + ring_in[(0 if d == 1 else 1, step - 1) + cut].astype(F32)
                    buf[where] = total.astype(buf.dtype)
                    copy = remote(
                        buf.at[where],
                        ring_in.at[(0 if d == 1 else 1, step) + cut],
                        phase,
                        i,
                        ring_slot(d, step),
                        beside[d],
                    )
                    ring[d, step, i] = copy
                    copies.append(copy)
        for i, (buf, sib, ring_in, cut, far) in enumerate(pieces):
            slot = slot_of(0)
            near[slot, i].wait_recv()
            total = buf[(me,) + cut].astype(F32) + sib[(slot,) + cut].astype(F32)
            for d in (1, -1):
                ring[d, reach - 1, i].wait_recv()
                total = total + ring_in[(0 if d == 1 else 1, reach - 1) + cut].astype(F32)
            buf[(me,) + cut] = total.astype(buf.dtype)
        for copy in copies:
            copy.wait_send()

    gathered[me, :, pl.ds(hd, kv_width)] = fresh_ref[:, 0, :]
    gathered[me, :, pl.ds(hd + kv_width, kv_width)] = fresh_ref[:, 1, :]
    probs = jnp.exp(score_ref[...].astype(F32) / 4.0)
    probs = probs / jnp.sum(probs, axis=0, keepdims=True)
    expert_of = lax.broadcasted_iota(jnp.int32, (LANES, row_dev), 0)
    gates = jnp.zeros((LANES, row_dev), F32)
    for k in range(ids_ref.shape[0]):
        gates = gates + jnp.where(ids_ref[k : k + 1, :] == expert_of, probs[k : k + 1, :], 0.0)
    gate_all[me] = gates.T
    loads[0].wait()
    pl.semaphore_wait(barrier, 3)
    every = (slice(None), slice(None))
    cuts = [(slice(None), pl.ds(c0, w)) for c0, w in halves(gathered.shape[-1], LANES)]
    gather(0, [(gathered, cuts[0], 1), (gathered, cuts[1], -1), (gate_all, every, 1)])

    owner_line = owner_ref[...]
    owner = jnp.broadcast_to(owner_line, (LANES, segs)).astype(F32).T.astype(jnp.int32)
    owner_col = owner[:, :1]
    blocks = segs // BLOCK_SEGS
    in_block = (
        lax.div(lax.broadcasted_iota(jnp.int32, (blocks, segs), 1), BLOCK_SEGS)
        == lax.broadcasted_iota(jnp.int32, (blocks, segs), 0)
    )
    lengths = jnp.where(in_block, length_ref[...].astype(F32), 0.0).astype(BF16)
    spread_shape = (segs, BLOCK_SEGS * slots)
    spread = (
        lax.rem(lax.broadcasted_iota(jnp.int32, spread_shape, 0), BLOCK_SEGS)
        == lax.div(lax.broadcasted_iota(jnp.int32, spread_shape, 1), slots)
    ).astype(BF16)
    live = jnp.dot(lengths, spread, preferred_element_type=F32)
    slot_id = lax.rem(lax.broadcasted_iota(jnp.int32, live.shape, 1), slots).astype(F32)
    bias_all = jnp.where(slot_id < live, 0.0, LOW)
    pick = (lax.broadcasted_iota(jnp.int32, (segs, rows), 1) == owner_col).astype(BF16)
    tile = 512

    def pick_queries(j, carry):
        cols = pl.ds(pl.multiple_of(j * tile, tile), tile)
        block = gathered[:, :, cols].reshape(rows, tile)
        seg_query[:, cols] = jnp.dot(pick, block, preferred_element_type=F32).astype(BF16)
        return carry

    lax.fori_loop(0, hd // tile, pick_queries, 0)
    loads[1].wait()
    loads[2].wait()

    wide = BLOCK_SEGS * slots
    tall = BLOCK_SEGS * group_size
    row_seg = lax.rem(lax.broadcasted_iota(jnp.int32, (tall, wide), 0), BLOCK_SEGS)
    col_seg = lax.div(lax.broadcasted_iota(jnp.int32, (tall, wide), 1), slots)
    same = row_seg == col_seg
    lane_of = lax.broadcasted_iota(jnp.int32, (BLOCK_SEGS, LANES), 1)
    scale = HEAD_SIZE ** (-0.5)
    stat_max = []
    stat_sum = []
    for b in range(blocks):
        span = pl.ds(b * BLOCK_SEGS, BLOCK_SEGS)
        bias = bias_all[b : b + 1]
        block_max = jnp.zeros((BLOCK_SEGS, LANES), F32)
        block_sum = jnp.zeros((BLOCK_SEGS, LANES), F32)
        for g in range(kv_heads):
            kcols = pl.ds(g * HEAD_SIZE, HEAD_SIZE)
            keys = key_v[span, :, kcols].reshape(wide, HEAD_SIZE)
            values = value_v[span, :, kcols].reshape(wide, HEAD_SIZE)
            stacked = jnp.concatenate(
                [
                    seg_query[span, pl.ds((g * group_size + h) * HEAD_SIZE, HEAD_SIZE)]
                    for h in range(group_size)
                ],
                axis=0,
            )
            scores = lax.dot_general(
                stacked, keys, (((1,), (1,)), ((), ())), preferred_element_type=F32
            )
            scores = jnp.where(same, scores * scale + bias, LOW)
            top = jnp.max(scores, axis=1, keepdims=True)
            prob = jnp.exp(scores - top)
            total = jnp.sum(prob, axis=1, keepdims=True)
            out = jnp.dot(prob.astype(BF16), values, preferred_element_type=F32)
            for h in range(group_size):
                head = g * group_size + h
                lines = slice(h * BLOCK_SEGS, (h + 1) * BLOCK_SEGS)
                seg_out[span, pl.ds(head * HEAD_SIZE, HEAD_SIZE)] = out[lines]
                block_max = jnp.where(lane_of == head, top[lines], block_max)
                block_sum = jnp.where(lane_of == head, total[lines], block_sum)
        stat_max.append(block_max)
        stat_sum.append(block_sum)
    seg_max = jnp.concatenate(stat_max, axis=0)
    seg_sum = jnp.concatenate(stat_sum, axis=0)

    place = lax.broadcasted_iota(jnp.int32, (segs, LANES), 0)

    def scan(value, combine, forward):
        sh = 1
        while sh < segs:
            amount = sh if forward else segs - sh
            moved = pltpu.roll(value, amount, 0)
            near = pltpu.roll(owner, amount, 0)
            inside = (place >= sh) if forward else (place < segs - sh)
            value = jnp.where(inside & (near == owner), combine(value, moved), value)
            sh *= 2
        return value

    row_max = scan(scan(seg_max, jnp.maximum, True), jnp.maximum, False)
    weight = jnp.exp(seg_max - row_max)
    row_sum = scan(seg_sum * weight, jnp.add, True)
    row_sum = jnp.maximum(scan(row_sum, jnp.maximum, False), 1.0)
    row_lse = row_max + jnp.log(row_sum)
    weight = weight / row_sum
    first = (place == 0) | (pltpu.roll(owner, 1, 0) != owner)
    lane = lax.broadcasted_iota(jnp.int32, (segs, LANES), 1)
    stats = jnp.where(lane == HQ, (owner + 1).astype(F32), row_lse)
    stats = jnp.where(first & (lane <= HQ), stats, 0.0)

    to_place = (lax.broadcasted_iota(jnp.int32, (segs, pos_lanes), 1) == owner_col + me).astype(F32)
    stats_t = jnp.dot(
        stats.T, to_place, precision=lax.Precision.HIGHEST, preferred_element_type=F32
    )
    spare = jnp.zeros((8 - per_dev - 1, pos_lanes), F32)
    for d in range(n):
        lse_tab[d] = jnp.concatenate(
            [stats_t[d * per_dev : (d + 1) * per_dev], stats_t[HQ : HQ + 1], spare], axis=0
        )
    put = (
        lax.broadcasted_iota(jnp.int32, (pos, segs), 0) == owner_line + me
    ).astype(BF16)
    for d in range(n):
        scaled = jnp.concatenate(
            [
                (
                    seg_out[:, pl.ds(head * HEAD_SIZE, HEAD_SIZE)] * weight[:, head : head + 1]
                ).astype(BF16)
                for head in range(d * per_dev, (d + 1) * per_dev)
            ],
            axis=1,
        )
        table[d] = jnp.dot(put, scaled, preferred_element_type=F32).astype(BF16)

    cuts = [(pl.ds(r0, c), slice(None)) for r0, c in halves(pos, 16)]
    scatter_sum(
        1,
        [
            (table, table_sib, table_ring, cuts[0], 1),
            (table, table_sib, table_ring, cuts[1], -1),
            (lse_tab, lse_sib, lse_ring, every, 1),
        ],
    )

    my_lse = lse_tab[me]
    my_table = table[me]
    row_of = my_lse[per_dev : per_dev + 1, :].astype(jnp.int32) - 1
    hit = lax.broadcasted_iota(jnp.int32, (rows, pos_lanes), 0) == row_of
    heads = []
    full = (slice(None), slice(None))
    for h in range(per_dev):
        head = me * per_dev + h
        g = lax.div(head, group_size)
        q_cols = pl.ds(pl.multiple_of(head * HEAD_SIZE, HEAD_SIZE), HEAD_SIZE)
        k_cols = pl.ds(pl.multiple_of(hd + g * HEAD_SIZE, HEAD_SIZE), HEAD_SIZE)
        v_cols = pl.ds(pl.multiple_of(hd + (kv_heads + g) * HEAD_SIZE, HEAD_SIZE), HEAD_SIZE)
        q = gathered[full + (q_cols,)].reshape(rows, HEAD_SIZE).astype(F32)
        k = gathered[full + (k_cols,)].reshape(rows, HEAD_SIZE).astype(F32)
        v = gathered[full + (v_cols,)].reshape(rows, HEAD_SIZE).astype(F32)
        own = jnp.sum(q * k, axis=1, keepdims=True) * scale
        lse = jnp.where(hit, my_lse[h : h + 1, :], LOW)
        top = jnp.maximum(jnp.max(lse, axis=1, keepdims=True), own)
        share = jnp.exp(lse - top)
        fresh = jnp.exp(own - top)
        inverse = 1.0 / (jnp.sum(share, axis=1, keepdims=True) + fresh)
        mixed_in = jnp.dot(
            (share * inverse)[:, :pos].astype(BF16),
            my_table[:, h * HEAD_SIZE : (h + 1) * HEAD_SIZE],
            preferred_element_type=F32,
        )
        heads.append((mixed_in + v * (fresh * inverse)).astype(BF16))
    attention = jnp.concatenate(heads, axis=1) if per_dev > 1 else heads[0]

    loads[4].wait()

    def project(j, carry):
        cols = pl.ds(pl.multiple_of(j * tile, tile), tile)
        product = jnp.dot(attention, proj_v[:, cols], preferred_element_type=F32)
        part[full + (cols,)] = product.astype(BF16).reshape(n, row_dev, tile)
        return carry

    lax.fori_loop(0, model // tile, project, 0)
    cuts = [(slice(None), pl.ds(c0, w)) for c0, w in halves(model, LANES)]
    part_pieces = [
        (part, part_sib, part_ring, cuts[0], 1),
        (part, part_sib, part_ring, cuts[1], -1),
    ]
    scatter_sum(2, part_pieces)

    loads[3].wait()
    mixed = (hidden_v[...].astype(F32) + part[me].astype(F32)).astype(BF16).astype(F32)
    scale_row = lax.rsqrt(jnp.mean(mixed * mixed, axis=1, keepdims=True) + 1e-06)
    normed_all[me] = (mixed * scale_row * gain_ref[...].astype(F32).reshape(1, model)).astype(BF16)
    gather(3, [(normed_all, cuts[0], 1), (normed_all, cuts[1], -1)])

    all_gates = gate_all[...].reshape(rows, LANES)
    gate_lane = lax.broadcasted_iota(jnp.int32, (rows, LANES), 1)
    gate = jnp.sum(jnp.where(gate_lane == me, all_gates, 0.0), axis=1, keepdims=True)
    loads[5].wait()
    loads[6].wait()
    ff_tile = 256

    def hidden_units(j, carry):
        cols = pl.ds(pl.multiple_of(j * ff_tile, ff_tile), ff_tile)
        tokens = normed_all[...].reshape(rows, model)
        gate_proj = jnp.dot(tokens, wg_v[:, cols], preferred_element_type=F32)
        up_proj = jnp.dot(tokens, wu_v[:, cols], preferred_element_type=F32)
        act_v[:, cols] = (jax.nn.silu(gate_proj) * up_proj).astype(BF16)
        return carry

    lax.fori_loop(0, ff // ff_tile, hidden_units, 0)
    loads[7].wait()

    def down(j, carry):
        cols = pl.ds(pl.multiple_of(j * tile, tile), tile)
        product = jnp.dot(act_v[...], wd_v[:, cols], preferred_element_type=F32)
        part[full + (cols,)] = (
            (product * gate).astype(BF16).reshape(n, row_dev, tile)
        )
        return carry

    lax.fori_loop(0, model // tile, down, 0)
    scatter_sum(4, part_pieces)
    out_ref[...] = (mixed + part[me].astype(F32)).astype(BF16)


def on_device(
    snake,
    hidden_in,
    queries,
    fresh_key_value,
    segment_key_cache,
    segment_value_cache,
    segment_owner_row,
    segment_length,
    expert_ids,
    gate_score,
    out_proj,
    norm_gain,
    w_gate,
    w_up,
    w_down,
):
    n = lax.axis_size("dev")
    chips = n // 2
    row_dev, model = hidden_in.shape
    segs, slots, kv_width = segment_key_cache.shape
    kv_heads = kv_width // HEAD_SIZE
    ff = w_gate.shape[2]
    per_dev = HQ // n
    rows = n * row_dev
    pos = rows + n
    pos_lanes = -(-pos // LANES) * LANES
    dims = (n, snake, row_dev, model, ff, segs, slots, kv_heads, per_dev, pos, pos_lanes)
    own_cols = per_dev * HEAD_SIZE
    hd = queries.shape[1]
    vmem = pl.BlockSpec(memory_space=pltpu.VMEM)
    hbm = pl.BlockSpec(memory_space=pl.ANY)
    return pl.pallas_call(
        functools.partial(layer_kernel, dims),
        out_shape=jax.ShapeDtypeStruct((row_dev, model), BF16),
        in_specs=[hbm, hbm, vmem, hbm, hbm] + [vmem] * 4 + [hbm, vmem, hbm, hbm, hbm],
        out_specs=vmem,
        scratch_shapes=[
            pltpu.VMEM(segment_key_cache.shape, BF16),
            pltpu.VMEM(segment_value_cache.shape, BF16),
            pltpu.VMEM(out_proj.shape, BF16),
            pltpu.VMEM(w_gate.shape[1:], BF16),
            pltpu.VMEM(w_up.shape[1:], BF16),
            pltpu.VMEM(w_down.shape[1:], BF16),
            pltpu.VMEM((row_dev, model), BF16),
            pltpu.SemaphoreType.DMA((8,)),
            pltpu.VMEM((n, row_dev, hd + 2 * kv_width), BF16),
            pltpu.VMEM((n, row_dev, LANES), F32),
            pltpu.VMEM((segs, hd), BF16),
            pltpu.VMEM((segs, hd), F32),
            pltpu.VMEM((n, pos, own_cols), BF16),
            pltpu.VMEM((chips, pos, own_cols), BF16),
            pltpu.VMEM((2, chips // 2, pos, own_cols), BF16),
            pltpu.VMEM((n, 8, pos_lanes), F32),
            pltpu.VMEM((chips, 8, pos_lanes), F32),
            pltpu.VMEM((2, chips // 2, 8, pos_lanes), F32),
            pltpu.VMEM((n, row_dev, model), BF16),
            pltpu.VMEM((chips, row_dev, model), BF16),
            pltpu.VMEM((2, chips // 2, row_dev, model), BF16),
            pltpu.VMEM((n, row_dev, model), BF16),
            pltpu.VMEM((rows, ff), BF16),
            pltpu.SemaphoreType.DMA((5, 3, 2 * chips)),
            pltpu.SemaphoreType.DMA((5, 3, 2 * chips)),
        ],
        compiler_params=pltpu.CompilerParams(
            collective_id=0, has_side_effects=True, vmem_limit_bytes=60 * 2**20
        ),
        name="decode_layer",
    )(
        hidden_in,
        queries,
        fresh_key_value,
        segment_key_cache,
        segment_value_cache,
        segment_owner_row.reshape(1, segs),
        segment_length.reshape(1, segs),
        expert_ids.T,
        gate_score.T,
        out_proj,
        norm_gain,
        w_gate,
        w_up,
        w_down,
    )


def snake_ring(mesh):
    places = [getattr(d, "coords", None) for d in mesh.devices.reshape(-1, mesh.shape["dev"])[0]]
    if any(p is None for p in places):
        return False
    places = [tuple(p) for p in places[::2]]
    return len(places) > 2 and len({p[1] for p in places}) == 2 and len({p[2] for p in places}) > 1


def solution(mesh):
    placed = (
        P(("groups", "dev"), None),
        P(("groups", "dev"), None),
        P(("groups", "dev"), None, None),
        P(("groups", "dev"), None, None),
        P(("groups", "dev"), None, None),
        P(("groups", "dev")),
        P(("groups", "dev")),
        P(("groups", "dev"), None),
        P(("groups", "dev"), None),
        P("dev", None),
        P(),
        P("dev", None, None),
        P("dev", None, None),
        P("dev", None, None),
    )
    return jax.shard_map(
        functools.partial(on_device, snake_ring(mesh)),
        mesh=mesh,
        in_specs=placed,
        out_specs=P(("groups", "dev"), None),
        check_vma=False,
    )
```

time: 138 us -> 112 us (0.81)
  Pallas kernels: 127 us -> 110 us
  local copies, waits for them, and re-layouts: 7.38 us -> 1.57 us
  other arithmetic: 2.71 us -> 0 us
    pallas_call x1, Pallas kernels: 127 us -> 110 us  [on_device(): pl.pallas_call(functools.partial(layer_kernel, dims), out_shape=jax.Shape...]
    unnamed x3 -> x1, local copies, waits for them, and re-layouts: 3.65 us -> 1.57 us
    reduce_sum x2 -> x0, other arithmetic: 1.41 us -> none  [the longest x1 0.71 us: on_device(): probs = probs / jnp.sum(probs, axis=1, keepdims=True)]
where the time goes in v2:
time: 112 us
  Pallas kernels  110 us (98%)
  local copies, waits for them, and re-layouts  1.57 us (1%)
    pallas_call x1, Pallas kernels, on_device(): pl.pallas_call(functools.partial(layer_kernel, dims), out_shape=jax.Shape...  110 us

profile of v2, /device:TPU:0, one launch (start us, length us, event | category | flops | bytes accessed | tf_op | source)
XLA Modules:
  0.0 111.9 jit_solution(16232358357285691756)
XLA Ops:
  0.0 110.3 %decode_layer.1 = bf16[16,4096]{1,0:T(8,128)(2,1)} custom-call(bf16[16,4096]{1,0:T(8,128)(2,1)} %hidden_hbm.1, bf16[16,4096]{1,0:T(8,128)(2,1)} %query_hbm.1, bf16[16,2,256]{2,1,0:T(2,128)(2,1)} %fresh_ref.1, bf16[128,16,256]{2,1,0:T(8,128)(2,1)} %key_hbm.1, bf16[128,16,256]{2,1,0:T(8,128)(2,1)} %value_hbm.1, s32[1,128]{1,0:T(1,128)} %bitcast.6, ...), custom_call_target="tpu_custom_call" | custom-call | tf_op jit(solution)/shard_map/decode_layer/pallas_call | solution.py:488
  110.3 1.6 %copy.16 = bf16[16,4096]{1,0:T(8,128)(2,1)} copy(bf16[16,4096]{1,0:T(8,128)(2,1)} %decode_layer.1) | data formatting | bytes 262144

commit v3 on v2

--- a/solution.py
+++ b/solution.py
@@ -60,6 +60,9 @@
     part_sib,
     part_ring,
     normed_all,
+    scale_all,
+    gate_acc,
+    up_acc,
     act_v,
     send_sem,
     recv_sem,
@@ -143,30 +146,32 @@
         ring = {}
         beside_me = []
 
-        def to_sibling(i, offset):
-            buf, cut, far = pieces[i]
+        def to_sibling(piece, offset):
+            number, buf, cut, far = piece
             ref = buf.at[(chip_at(offset) * 2 + core,) + cut]
-            copy = remote(ref, ref, phase, i, slot_of(offset), sibling)
+            copy = remote(ref, ref, phase, number, slot_of(offset), sibling)
             copies.append(copy)
             beside_me.append(copy)
 
         for step in range(reach):
-            for i, (buf, cut, far) in enumerate(pieces):
+            for number, buf, cut, far in pieces:
                 for d in (1, -1):
                     if step > 0:
-                        ring[d, step - 1, i].wait_recv()
+                        ring[d, step - 1, number].wait_recv()
                     if step == reach - 1 and far != d:
                         continue
                     ref = buf.at[(chip_at(-d * step) * 2 + core,) + cut]
-                    copy = remote(ref, ref, phase, i, ring_slot(d, step), beside[d])
-                    ring[d, step, i] = copy
+                    copy = remote(ref, ref, phase, number, ring_slot(d, step), beside[d])
+                    ring[d, step, number] = copy
                     copies.append(copy)
-            for i in range(len(pieces)):
+            for piece in pieces:
                 for offset in (step, -step) if step else (0,):
-                    to_sibling(i, offset)
-        for i, (buf, cut, far) in enumerate(pieces):
-            ring[far, reach - 1, i].wait_recv()
-            to_sibling(i, reach)
+                    to_sibling(piece, offset)
+            yield
+        for piece in pieces:
+            ring[piece[3], reach - 1, piece[0]].wait_recv()
+            to_sibling(piece, reach)
+        yield
         for copy in beside_me:
             copy.wait_recv()
         for copy in copies:
@@ -177,52 +182,64 @@
         ring = {}
         near = {}
         for offset in offsets:
-            for i, (buf, sib, ring_in, cut, far) in enumerate(pieces):
+            for number, buf, sib, ring_in, cut, far in pieces:
                 slot = slot_of(offset)
                 copy = remote(
                     buf.at[(chip_at(offset) * 2 + 1 - core,) + cut],
                     sib.at[(slot,) + cut],
                     phase,
-                    i,
+                    number,
                     slot,
                     sibling,
                 )
                 copies.append(copy)
-                near[slot, i] = copy
+                near[slot, number] = copy
+        yield
         for step in range(reach):
-            for i, (buf, sib, ring_in, cut, far) in enumerate(pieces):
+            for number, buf, sib, ring_in, cut, far in pieces:
                 for d in (1, -1):
                     if step == 0 and far != d:
                         continue
                     offset = d * (reach - step)
                     slot = slot_of(offset)
                     where = (chip_at(offset) * 2 + core,) + cut
-                    near[slot, i].wait_recv()
+                    near[slot, number].wait_recv()
                     total = buf[where].astype(F32) + sib[(slot,) + cut].astype(F32)
-                    if (d, step - 1, i) in ring:
-                        ring[d, step - 1, i].wait_recv()
+                    if (d, step - 1, number) in ring:
+                        ring[d, step - 1, number].wait_recv()
                         total = total + ring_in[(0 if d == 1 else 1, step - 1) + cut].astype(F32)
                     buf[where] = total.astype(buf.dtype)
                     copy = remote(
                         buf.at[where],
                         ring_in.at[(0 if d == 1 else 1, step) + cut],
                         phase,
-                        i,
+                        number,
                         ring_slot(d, step),
                         beside[d],
                     )
-                    ring[d, step, i] = copy
+                    ring[d, step, number] = copy
                     copies.append(copy)
-        for i, (buf, sib, ring_in, cut, far) in enumerate(pieces):
+            yield
+        for number, buf, sib, ring_in, cut, far in pieces:
             slot = slot_of(0)
-            near[slot, i].wait_recv()
+            near[slot, number].wait_recv()
             total = buf[(me,) + cut].astype(F32) + sib[(slot,) + cut].astype(F32)
             for d in (1, -1):
-                ring[d, reach - 1, i].wait_recv()
+                ring[d, reach - 1, number].wait_recv()
                 total = total + ring_in[(0 if d == 1 else 1, reach - 1) + cut].astype(F32)
             buf[(me,) + cut] = total.astype(buf.dtype)
         for copy in copies:
             copy.wait_send()
+
+    def drive(streams, lag):
+        streams = list(streams)
+        active = [True] * len(streams)
+        turn = 0
+        while any(active):
+            for i, stream in enumerate(streams):
+                if active[i] and turn >= lag * i:
+                    active[i] = next(stream, "end") != "end"
+            turn += 1
 
     gathered[me, :, pl.ds(hd, kv_width)] = fresh_ref[:, 0, :]
     gathered[me, :, pl.ds(hd + kv_width, kv_width)] = fresh_ref[:, 1, :]
@@ -236,8 +253,6 @@
     loads[0].wait()
     pl.semaphore_wait(barrier, 3)
     every = (slice(None), slice(None))
-    cuts = [(slice(None), pl.ds(c0, w)) for c0, w in halves(gathered.shape[-1], LANES)]
-    gather(0, [(gathered, cuts[0], 1), (gathered, cuts[1], -1), (gate_all, every, 1)])
 
     owner_line = owner_ref[...]
     owner = jnp.broadcast_to(owner_line, (LANES, segs)).astype(F32).T.astype(jnp.int32)
@@ -265,10 +280,6 @@
         seg_query[:, cols] = jnp.dot(pick, block, preferred_element_type=F32).astype(BF16)
         return carry
 
-    lax.fori_loop(0, hd // tile, pick_queries, 0)
-    loads[1].wait()
-    loads[2].wait()
-
     wide = BLOCK_SEGS * slots
     tall = BLOCK_SEGS * group_size
     row_seg = lax.rem(lax.broadcasted_iota(jnp.int32, (tall, wide), 0), BLOCK_SEGS)
@@ -276,40 +287,60 @@
     same = row_seg == col_seg
     lane_of = lax.broadcasted_iota(jnp.int32, (BLOCK_SEGS, LANES), 1)
     scale = HEAD_SIZE ** (-0.5)
-    stat_max = []
-    stat_sum = []
-    for b in range(blocks):
+    stat_max = [jnp.zeros((BLOCK_SEGS, LANES), F32)] * blocks
+    stat_sum = [jnp.zeros((BLOCK_SEGS, LANES), F32)] * blocks
+
+    def attend(b, g):
         span = pl.ds(b * BLOCK_SEGS, BLOCK_SEGS)
-        bias = bias_all[b : b + 1]
-        block_max = jnp.zeros((BLOCK_SEGS, LANES), F32)
-        block_sum = jnp.zeros((BLOCK_SEGS, LANES), F32)
-        for g in range(kv_heads):
-            kcols = pl.ds(g * HEAD_SIZE, HEAD_SIZE)
-            keys = key_v[span, :, kcols].reshape(wide, HEAD_SIZE)
-            values = value_v[span, :, kcols].reshape(wide, HEAD_SIZE)
-            stacked = jnp.concatenate(
-                [
-                    seg_query[span, pl.ds((g * group_size + h) * HEAD_SIZE, HEAD_SIZE)]
-                    for h in range(group_size)
-                ],
-                axis=0,
-            )
-            scores = lax.dot_general(
-                stacked, keys, (((1,), (1,)), ((), ())), preferred_element_type=F32
-            )
-            scores = jnp.where(same, scores * scale + bias, LOW)
-            top = jnp.max(scores, axis=1, keepdims=True)
-            prob = jnp.exp(scores - top)
-            total = jnp.sum(prob, axis=1, keepdims=True)
-            out = jnp.dot(prob.astype(BF16), values, preferred_element_type=F32)
-            for h in range(group_size):
-                head = g * group_size + h
-                lines = slice(h * BLOCK_SEGS, (h + 1) * BLOCK_SEGS)
-                seg_out[span, pl.ds(head * HEAD_SIZE, HEAD_SIZE)] = out[lines]
-                block_max = jnp.where(lane_of == head, top[lines], block_max)
-                block_sum = jnp.where(lane_of == head, total[lines], block_sum)
-        stat_max.append(block_max)
-        stat_sum.append(block_sum)
+        kcols = pl.ds(g * HEAD_SIZE, HEAD_SIZE)
+        keys = key_v[span, :, kcols].reshape(wide, HEAD_SIZE)
+        values = value_v[span, :, kcols].reshape(wide, HEAD_SIZE)
+        stacked = jnp.concatenate(
+            [
+                seg_query[span, pl.ds((g * group_size + h) * HEAD_SIZE, HEAD_SIZE)]
+                for h in range(group_size)
+            ],
+            axis=0,
+        )
+        scores = lax.dot_general(
+            stacked, keys, (((1,), (1,)), ((), ())), preferred_element_type=F32
+        )
+        scores = jnp.where(same, scores * scale + bias_all[b : b + 1], LOW)
+        top = jnp.max(scores, axis=1, keepdims=True)
+        prob = jnp.exp(scores - top)
+        total = jnp.sum(prob, axis=1, keepdims=True)
+        out = jnp.dot(prob.astype(BF16), values, preferred_element_type=F32)
+        for h in range(group_size):
+            head = g * group_size + h
+            lines = slice(h * BLOCK_SEGS, (h + 1) * BLOCK_SEGS)
+            seg_out[span, pl.ds(head * HEAD_SIZE, HEAD_SIZE)] = out[lines]
+            stat_max[b] = jnp.where(lane_of == head, top[lines], stat_max[b])
+            stat_sum[b] = jnp.where(lane_of == head, total[lines], stat_sum[b])
+
+    group_cols = group_size * HEAD_SIZE
+
+    def query_stream(g):
+        start = g * group_cols
+        extent = group_cols
+        if g == kv_heads - 1:
+            extent += 2 * kv_width
+        cuts = [
+            (slice(None), pl.ds(start + c0, w)) for c0, w in halves(extent, LANES)
+        ]
+        pieces = [(2 * g, gathered, cuts[0], 1), (2 * g + 1, gathered, cuts[1], -1)]
+        if g == kv_heads - 1:
+            pieces.append((2 * kv_heads, gate_all, every, 1))
+        yield from gather(0, pieces)
+        lax.fori_loop(g * group_cols // tile, (g + 1) * group_cols // tile, pick_queries, 0)
+        if g == 0:
+            loads[1].wait()
+            loads[2].wait()
+        for b in range(blocks):
+            attend(b, g)
+            if b % 2:
+                yield
+
+    drive([query_stream(g) for g in range(kv_heads)], 2)
     seg_max = jnp.concatenate(stat_max, axis=0)
     seg_sum = jnp.concatenate(stat_sum, axis=0)
 
@@ -349,35 +380,27 @@
     put = (
         lax.broadcasted_iota(jnp.int32, (pos, segs), 0) == owner_line + me
     ).astype(BF16)
-    for d in range(n):
-        scaled = jnp.concatenate(
-            [
-                (
-                    seg_out[:, pl.ds(head * HEAD_SIZE, HEAD_SIZE)] * weight[:, head : head + 1]
-                ).astype(BF16)
-                for head in range(d * per_dev, (d + 1) * per_dev)
-            ],
-            axis=1,
-        )
-        table[d] = jnp.dot(put, scaled, preferred_element_type=F32).astype(BF16)
-
-    cuts = [(pl.ds(r0, c), slice(None)) for r0, c in halves(pos, 16)]
-    scatter_sum(
-        1,
-        [
-            (table, table_sib, table_ring, cuts[0], 1),
-            (table, table_sib, table_ring, cuts[1], -1),
-            (lse_tab, lse_sib, lse_ring, every, 1),
-        ],
-    )
-
-    my_lse = lse_tab[me]
-    my_table = table[me]
-    row_of = my_lse[per_dev : per_dev + 1, :].astype(jnp.int32) - 1
-    hit = lax.broadcasted_iota(jnp.int32, (rows, pos_lanes), 0) == row_of
-    heads = []
+    weight_of = [weight[:, head : head + 1] for head in range(HQ)]
+    table_cuts = halves(pos, 16)
+
+    def fill_table(h):
+        for d in range(n):
+            head = d * per_dev + h
+            scaled = (
+                seg_out[:, pl.ds(head * HEAD_SIZE, HEAD_SIZE)] * weight_of[head]
+            ).astype(BF16)
+            table[d, :, pl.ds(h * HEAD_SIZE, HEAD_SIZE)] = jnp.dot(
+                put, scaled, preferred_element_type=F32
+            ).astype(BF16)
+
+    heads = [None] * per_dev
     full = (slice(None), slice(None))
-    for h in range(per_dev):
+
+    def combine(h):
+        my_lse = lse_tab[me]
+        my_table = table[me, :, pl.ds(h * HEAD_SIZE, HEAD_SIZE)]
+        row_of = my_lse[per_dev : per_dev + 1, :].astype(jnp.int32) - 1
+        hit = lax.broadcasted_iota(jnp.int32, (rows, pos_lanes), 0) == row_of
         head = me * per_dev + h
         g = lax.div(head, group_size)
         q_cols = pl.ds(pl.multiple_of(head * HEAD_SIZE, HEAD_SIZE), HEAD_SIZE)
@@ -393,11 +416,23 @@
         fresh = jnp.exp(own - top)
         inverse = 1.0 / (jnp.sum(share, axis=1, keepdims=True) + fresh)
         mixed_in = jnp.dot(
-            (share * inverse)[:, :pos].astype(BF16),
-            my_table[:, h * HEAD_SIZE : (h + 1) * HEAD_SIZE],
-            preferred_element_type=F32,
+            (share * inverse)[:, :pos].astype(BF16), my_table, preferred_element_type=F32
         )
-        heads.append((mixed_in + v * (fresh * inverse)).astype(BF16))
+        heads[h] = (mixed_in + v * (fresh * inverse)).astype(BF16)
+
+    def table_stream(h):
+        fill_table(h)
+        cols = pl.ds(h * HEAD_SIZE, HEAD_SIZE)
+        pieces = [
+            (2 * h + i, table, table_sib, table_ring, (pl.ds(r0, c), cols), far)
+            for i, ((r0, c), far) in enumerate(zip(table_cuts, (1, -1)))
+        ]
+        if h == 0:
+            pieces.append((2 * per_dev, lse_tab, lse_sib, lse_ring, every, 1))
+        yield from scatter_sum(1, pieces)
+        combine(h)
+
+    drive([table_stream(h) for h in range(per_dev)], 1)
     attention = jnp.concatenate(heads, axis=1) if per_dev > 1 else heads[0]
 
     loads[4].wait()
@@ -408,36 +443,67 @@
         part[full + (cols,)] = product.astype(BF16).reshape(n, row_dev, tile)
         return carry
 
-    lax.fori_loop(0, model // tile, project, 0)
-    cuts = [(slice(None), pl.ds(c0, w)) for c0, w in halves(model, LANES)]
-    part_pieces = [
-        (part, part_sib, part_ring, cuts[0], 1),
-        (part, part_sib, part_ring, cuts[1], -1),
-    ]
-    scatter_sum(2, part_pieces)
-
-    loads[3].wait()
-    mixed = (hidden_v[...].astype(F32) + part[me].astype(F32)).astype(BF16).astype(F32)
-    scale_row = lax.rsqrt(jnp.mean(mixed * mixed, axis=1, keepdims=True) + 1e-06)
-    normed_all[me] = (mixed * scale_row * gain_ref[...].astype(F32).reshape(1, model)).astype(BF16)
-    gather(3, [(normed_all, cuts[0], 1), (normed_all, cuts[1], -1)])
+    stream_cols = [(c0, w) for c0, w in halves(model, tile)]
+
+    def part_pieces(i):
+        c0, w = stream_cols[i]
+        return [
+            (2 * i + j, part, part_sib, part_ring, (slice(None), pl.ds(c0 + at, width)), far)
+            for j, ((at, width), far) in enumerate(zip(halves(w, LANES), (1, -1)))
+        ]
+
+    mixed_of = [None] * len(stream_cols)
+    ff_tile = 256
+
+    def middle_stream(i):
+        c0, w = stream_cols[i]
+        cols = pl.ds(c0, w)
+        lax.fori_loop(c0 // tile, (c0 + w) // tile, project, 0)
+        yield from scatter_sum(2, part_pieces(i))
+        if i == 0:
+            loads[3].wait()
+        mixed = hidden_v[:, cols].astype(F32) + part[me, :, cols].astype(F32)
+        mixed = mixed.astype(BF16).astype(F32)
+        mixed_of[i] = mixed
+        gain = gain_ref[cols].astype(F32).reshape(1, w)
+        normed_all[me, :, cols] = (mixed * gain).astype(BF16)
+        pieces = [
+            (2 * i + j, normed_all, (slice(None), pl.ds(c0 + at, width)), far)
+            for j, ((at, width), far) in enumerate(zip(halves(w, LANES), (1, -1)))
+        ]
+        if i == len(stream_cols) - 1:
+            squares = sum(jnp.sum(m * m, axis=1, keepdims=True) for m in mixed_of)
+            scale_all[me] = jnp.broadcast_to(
+                lax.rsqrt(squares / model + 1e-06), (row_dev, LANES)
+            )
+            pieces.append((2 * len(stream_cols), scale_all, every, 1))
+        yield from gather(3, pieces)
+        if i == 0:
+            loads[5].wait()
+            loads[6].wait()
+        for j in range(ff // ff_tile):
+            units = pl.ds(j * ff_tile, ff_tile)
+            tokens = normed_all[:, :, cols].reshape(rows, w)
+            gate_proj = jnp.dot(tokens, wg_v[cols, units], preferred_element_type=F32)
+            up_proj = jnp.dot(tokens, wu_v[cols, units], preferred_element_type=F32)
+            if i > 0:
+                gate_proj = gate_proj + gate_acc[:, units]
+                up_proj = up_proj + up_acc[:, units]
+            if i < len(stream_cols) - 1:
+                gate_acc[:, units] = gate_proj
+                up_acc[:, units] = up_proj
+                yield
+            else:
+                row_scale = scale_all[...].reshape(rows, LANES)[:, :1]
+                gate_proj = gate_proj * row_scale
+                up_proj = up_proj * row_scale
+                act_v[:, units] = (jax.nn.silu(gate_proj) * up_proj).astype(BF16)
+
+    drive([middle_stream(i) for i in range(len(stream_cols))], 2)
 
     all_gates = gate_all[...].reshape(rows, LANES)
     gate_lane = lax.broadcasted_iota(jnp.int32, (rows, LANES), 1)
     gate = jnp.sum(jnp.where(gate_lane == me, all_gates, 0.0), axis=1, keepdims=True)
-    loads[5].wait()
-    loads[6].wait()
-    ff_tile = 256
-
-    def hidden_units(j, carry):
-        cols = pl.ds(pl.multiple_of(j * ff_tile, ff_tile), ff_tile)
-        tokens = normed_all[...].reshape(rows, model)
-        gate_proj = jnp.dot(tokens, wg_v[:, cols], preferred_element_type=F32)
-        up_proj = jnp.dot(tokens, wu_v[:, cols], preferred_element_type=F32)
-        act_v[:, cols] = (jax.nn.silu(gate_proj) * up_proj).astype(BF16)
-        return carry
-
-    lax.fori_loop(0, ff // ff_tile, hidden_units, 0)
     loads[7].wait()
 
     def down(j, carry):
@@ -448,9 +514,14 @@
         )
         return carry
 
-    lax.fori_loop(0, model // tile, down, 0)
-    scatter_sum(4, part_pieces)
-    out_ref[...] = (mixed + part[me].astype(F32)).astype(BF16)
+    def out_stream(i):
+        c0, w = stream_cols[i]
+        lax.fori_loop(c0 // tile, (c0 + w) // tile, down, 0)
+        yield from scatter_sum(4, part_pieces(i))
+        cols = pl.ds(c0, w)
+        out_ref[:, cols] = (mixed_of[i] + part[me, :, cols].astype(F32)).astype(BF16)
+
+    drive([out_stream(i) for i in range(len(stream_cols))], 1)
 
 
 def on_device(
@@ -513,12 +584,15 @@
             pltpu.VMEM((chips, row_dev, model), BF16),
             pltpu.VMEM((2, chips // 2, row_dev, model), BF16),
             pltpu.VMEM((n, row_dev, model), BF16),
+            pltpu.VMEM((n, row_dev, LANES), F32),
+            pltpu.VMEM((rows, ff), F32),
+            pltpu.VMEM((rows, ff), F32),
             pltpu.VMEM((rows, ff), BF16),
-            pltpu.SemaphoreType.DMA((5, 3, 2 * chips)),
-            pltpu.SemaphoreType.DMA((5, 3, 2 * chips)),
+            pltpu.SemaphoreType.DMA((5, 5, 2 * chips)),
+            pltpu.SemaphoreType.DMA((5, 5, 2 * chips)),
         ],
         compiler_params=pltpu.CompilerParams(
-            collective_id=0, has_side_effects=True, vmem_limit_bytes=60 * 2**20
+            collective_id=0, has_side_effects=True, vmem_limit_bytes=62 * 2**20
         ),
         name="decode_layer",
     )(

time: 112 us -> 116 us (1.036)
  Pallas kernels: 110 us -> 115 us
    pallas_call x1, Pallas kernels: 110 us -> 115 us  [on_device(): pl.pallas_call(functools.partial(layer_kernel, dims), out_shape=jax.Shape...]
where the time goes in v3:
time: 116 us
  Pallas kernels  115 us (99%)
  local copies, waits for them, and re-layouts  1.57 us (1%)
    pallas_call x1, Pallas kernels, on_device(): pl.pallas_call(functools.partial(layer_kernel, dims), out_shape=jax.Shape...  115 us

profile of v3, /device:TPU:0, one launch (start us, length us, event | category | flops | bytes accessed | tf_op | source)
XLA Modules:
  0.0 116.2 jit_solution(4956306019092643251)
XLA Ops:
  0.0 114.6 %decode_layer.1 = bf16[16,4096]{1,0:T(8,128)(2,1)} custom-call(bf16[16,4096]{1,0:T(8,128)(2,1)} %hidden_hbm.1, bf16[16,4096]{1,0:T(8,128)(2,1)} %query_hbm.1, bf16[16,2,256]{2,1,0:T(2,128)(2,1)} %fresh_ref.1, bf16[128,16,256]{2,1,0:T(8,128)(2,1)} %key_hbm.1, bf16[128,16,256]{2,1,0:T(8,128)(2,1)} %value_hbm.1, s32[1,128]{1,0:T(1,128)} %bitcast.6, ...), custom_call_target="tpu_custom_call" | custom-call | tf_op jit(solution)/shard_map/decode_layer/pallas_call | solution.py:559
  114.6 1.6 %copy.16 = bf16[16,4096]{1,0:T(8,128)(2,1)} copy(bf16[16,4096]{1,0:T(8,128)(2,1)} %decode_layer.1) | data formatting | bytes 262144

commit v4 on v2

--- a/solution.py
+++ b/solution.py
@@ -47,7 +47,6 @@
     hidden_v,
     load_sem,
     gathered,
-    gate_all,
     seg_query,
     seg_out,
     table,
@@ -92,21 +91,33 @@
 
     sibling = chip * 2 + 1 - core
     beside = {d: chip_at(d) * 2 + core for d in (1, -1)}
-    offsets = [reach]
-    for dist in range(reach - 1, 0, -1):
-        offsets += [dist, -dist]
-    offsets.append(0)
+    near = list(range(1, reach - 1)) + [-dist for dist in range(reach - 2, 0, -1)]
+    far_away = [reach - 1, reach, 1 - reach]
+    offsets = [0] + near + far_away
+    near_slots = pl.ds(1, len(near))
+    far_slots = pl.ds(1 + len(near), len(far_away))
+    not_far = pl.ds(0, 1 + len(near))
 
     def slot_of(offset):
         return offsets.index(reach if offset == -reach else offset)
 
     def ring_slot(d, step):
-        return chips + (0 if d == 1 else reach) + step
+        return 4 + (0 if d == 1 else reach) + step
+
+    places = [chip_at(o) * 2 + c for c in (core, 1 - core) for o in offsets]
+
+    def row_ids(shape, axis):
+        index = lax.broadcasted_iota(jnp.int32, shape, axis)
+        chunk = lax.div(index, row_dev)
+        found = jnp.zeros(shape, jnp.int32)
+        for s, device in enumerate(places):
+            found = jnp.where(chunk == s, device * row_dev, found)
+        return found + lax.rem(index, row_dev)
 
     loads = []
     for i, (src, dst) in enumerate(
         [
-            (query_hbm, gathered.at[me, :, pl.ds(0, hd)]),
+            (query_hbm, gathered.at[0, 0, :, pl.ds(0, hd)]),
             (key_hbm, key_v),
             (value_hbm, value_v),
             (hidden_hbm, hidden_v),
@@ -138,74 +149,26 @@
         copy.start()
         return copy
 
-    def gather(phase, pieces):
+    def gather(phase, buf, cuts):
         copies = []
         ring = {}
         beside_me = []
 
-        def to_sibling(i, offset):
-            buf, cut, far = pieces[i]
-            ref = buf.at[(chip_at(offset) * 2 + core,) + cut]
-            copy = remote(ref, ref, phase, i, slot_of(offset), sibling)
+        def to_sibling(number, span):
+            copy = remote(buf.at[0, span], buf.at[1, span], phase, 0, number, sibling)
             copies.append(copy)
             beside_me.append(copy)
 
         for step in range(reach):
-            for i, (buf, cut, far) in enumerate(pieces):
+            for i, cut in enumerate(cuts):
                 for d in (1, -1):
                     if step > 0:
                         ring[d, step - 1, i].wait_recv()
-                    if step == reach - 1 and far != d:
+                    if step == reach - 1 and d != 1 - 2 * i:
                         continue
-                    ref = buf.at[(chip_at(-d * step) * 2 + core,) + cut]
-                    copy = remote(ref, ref, phase, i, ring_slot(d, step), beside[d])
-                    ring[d, step, i] = copy
-                    copies.append(copy)
-            for i in range(len(pieces)):
-                for offset in (step, -step) if step else (0,):
-                    to_sibling(i, offset)
-        for i, (buf, cut, far) in enumerate(pieces):
-            ring[far, reach - 1, i].wait_recv()
-            to_sibling(i, reach)
-        for copy in beside_me:
-            copy.wait_recv()
-        for copy in copies:
-            copy.wait_send()
-
-    def scatter_sum(phase, pieces):
-        copies = []
-        ring = {}
-        near = {}
-        for offset in offsets:
-            for i, (buf, sib, ring_in, cut, far) in enumerate(pieces):
-                slot = slot_of(offset)
-                copy = remote(
-                    buf.at[(chip_at(offset) * 2 + 1 - core,) + cut],
-                    sib.at[(slot,) + cut],
-                    phase,
-                    i,
-                    slot,
-                    sibling,
-                )
-                copies.append(copy)
-                near[slot, i] = copy
-        for step in range(reach):
-            for i, (buf, sib, ring_in, cut, far) in enumerate(pieces):
-                for d in (1, -1):
-                    if step == 0 and far != d:
-                        continue
-                    offset = d * (reach - step)
-                    slot = slot_of(offset)
-                    where = (chip_at(offset) * 2 + core,) + cut
-                    near[slot, i].wait_recv()
-                    total = buf[where].astype(F32) + sib[(slot,) + cut].astype(F32)
-                    if (d, step - 1, i) in ring:
-                        ring[d, step - 1, i].wait_recv()
-                        total = total + ring_in[(0 if d == 1 else 1, step - 1) + cut].astype(F32)
-                    buf[where] = total.astype(buf.dtype)
                     copy = remote(
-                        buf.at[where],
-                        ring_in.at[(0 if d == 1 else 1, step) + cut],
+                        buf.at[(0, slot_of(-d * step)) + cut],
+                        buf.at[(0, slot_of(-d * (step + 1))) + cut],
                         phase,
                         i,
                         ring_slot(d, step),
@@ -213,31 +176,87 @@
                     )
                     ring[d, step, i] = copy
                     copies.append(copy)
-        for i, (buf, sib, ring_in, cut, far) in enumerate(pieces):
-            slot = slot_of(0)
-            near[slot, i].wait_recv()
-            total = buf[(me,) + cut].astype(F32) + sib[(slot,) + cut].astype(F32)
-            for d in (1, -1):
-                ring[d, reach - 1, i].wait_recv()
-                total = total + ring_in[(0 if d == 1 else 1, reach - 1) + cut].astype(F32)
-            buf[(me,) + cut] = total.astype(buf.dtype)
+            if step == 0:
+                to_sibling(0, pl.ds(0, 1))
+            if step == reach - 2:
+                to_sibling(1, near_slots)
+        for i in range(len(cuts)):
+            ring[1 - 2 * i, reach - 1, i].wait_recv()
+        to_sibling(2, far_slots)
+        for copy in beside_me:
+            copy.wait_recv()
         for copy in copies:
             copy.wait_send()
 
-    gathered[me, :, pl.ds(hd, kv_width)] = fresh_ref[:, 0, :]
-    gathered[me, :, pl.ds(hd + kv_width, kv_width)] = fresh_ref[:, 1, :]
+    def scatter_sum(phase, arrays):
+        copies = []
+        ring = {}
+        crossing = {}
+        pieces = []
+        for a, (buf, sib, ring_in, cuts) in enumerate(arrays):
+            for number, span in enumerate((far_slots, not_far)):
+                copy = remote(
+                    buf.at[1, span], sib.at[span], phase, 2 * a, number, sibling
+                )
+                copies.append(copy)
+                crossing[a, number] = copy
+            for i, cut in enumerate(cuts):
+                pieces.append((a, buf, sib, ring_in, cut, 2 * a + i, 1 - 2 * i))
+
+        def crossed(a, number):
+            if (a, number) in crossing:
+                crossing.pop((a, number)).wait_recv()
+
+        for step in range(reach):
+            for a, buf, sib, ring_in, cut, number, far in pieces:
+                crossed(a, 0 if step < 2 else 1)
+                for d in (1, -1):
+                    if step == 0 and far != d:
+                        continue
+                    slot = slot_of(d * (reach - step))
+                    where = (0, slot) + cut
+                    total = buf[where].astype(F32) + sib[(slot,) + cut].astype(F32)
+                    if (d, step - 1, number) in ring:
+                        ring[d, step - 1, number].wait_recv()
+                        total = total + ring_in[(0 if d == 1 else 1, step - 1) + cut].astype(F32)
+                    buf[where] = total.astype(buf.dtype)
+                    copy = remote(
+                        buf.at[where],
+                        ring_in.at[(0 if d == 1 else 1, step) + cut],
+                        phase,
+                        number,
+                        ring_slot(d, step),
+                        beside[d],
+                    )
+                    ring[d, step, number] = copy
+                    copies.append(copy)
+        for a, buf, sib, ring_in, cut, number, far in pieces:
+            total = buf[(0, 0) + cut].astype(F32) + sib[(0,) + cut].astype(F32)
+            for d in (1, -1):
+                ring[d, reach - 1, number].wait_recv()
+                total = total + ring_in[(0 if d == 1 else 1, reach - 1) + cut].astype(F32)
+            buf[(0, 0) + cut] = total.astype(buf.dtype)
+        for copy in copies:
+            copy.wait_send()
+
+    gathered[0, 0, :, pl.ds(hd, kv_width)] = fresh_ref[:, 0, :]
+    gathered[0, 0, :, pl.ds(hd + kv_width, kv_width)] = fresh_ref[:, 1, :]
     probs = jnp.exp(score_ref[...].astype(F32) / 4.0)
     probs = probs / jnp.sum(probs, axis=0, keepdims=True)
     expert_of = lax.broadcasted_iota(jnp.int32, (LANES, row_dev), 0)
     gates = jnp.zeros((LANES, row_dev), F32)
     for k in range(ids_ref.shape[0]):
         gates = gates + jnp.where(ids_ref[k : k + 1, :] == expert_of, probs[k : k + 1, :], 0.0)
-    gate_all[me] = gates.T
+    gates = gates.T
+    rounded = gates.astype(BF16).astype(F32)
+    rest = pltpu.roll(gates - rounded, LANES // 2, 1)
+    lane_id = lax.broadcasted_iota(jnp.int32, (row_dev, LANES), 1)
+    gathered[0, 0, :, pl.ds(hd + 2 * kv_width, LANES)] = jnp.where(
+        lane_id < LANES // 2, rounded, rest
+    ).astype(BF16)
     loads[0].wait()
     pl.semaphore_wait(barrier, 3)
-    every = (slice(None), slice(None))
-    cuts = [(slice(None), pl.ds(c0, w)) for c0, w in halves(gathered.shape[-1], LANES)]
-    gather(0, [(gathered, cuts[0], 1), (gathered, cuts[1], -1), (gate_all, every, 1)])
+    gather(0, gathered, [(slice(None), pl.ds(c0, w)) for c0, w in halves(gathered.shape[-1], LANES)])
 
     owner_line = owner_ref[...]
     owner = jnp.broadcast_to(owner_line, (LANES, segs)).astype(F32).T.astype(jnp.int32)
@@ -256,12 +275,12 @@
     live = jnp.dot(lengths, spread, preferred_element_type=F32)
     slot_id = lax.rem(lax.broadcasted_iota(jnp.int32, live.shape, 1), slots).astype(F32)
     bias_all = jnp.where(slot_id < live, 0.0, LOW)
-    pick = (lax.broadcasted_iota(jnp.int32, (segs, rows), 1) == owner_col).astype(BF16)
+    pick = (row_ids((segs, rows), 1) == owner_col).astype(BF16)
     tile = 512
 
     def pick_queries(j, carry):
         cols = pl.ds(pl.multiple_of(j * tile, tile), tile)
-        block = gathered[:, :, cols].reshape(rows, tile)
+        block = gathered[:, :, :, cols].reshape(rows, tile)
         seg_query[:, cols] = jnp.dot(pick, block, preferred_element_type=F32).astype(BF16)
         return carry
 
@@ -341,42 +360,47 @@
     stats_t = jnp.dot(
         stats.T, to_place, precision=lax.Precision.HIGHEST, preferred_element_type=F32
     )
-    spare = jnp.zeros((8 - per_dev - 1, pos_lanes), F32)
-    for d in range(n):
-        lse_tab[d] = jnp.concatenate(
-            [stats_t[d * per_dev : (d + 1) * per_dev], stats_t[HQ : HQ + 1], spare], axis=0
-        )
+    stat_id = lax.broadcasted_iota(jnp.int32, (n * 8, LANES), 0)
+    stat_chunk, stat_id = lax.div(stat_id, 8), lax.rem(stat_id, 8)
+    wanted = jnp.full((n * 8, LANES), -1, jnp.int32)
+    for s, device in enumerate(places):
+        wanted = jnp.where(stat_chunk == s, device * per_dev + stat_id, wanted)
+    wanted = jnp.where(stat_id < per_dev, wanted, jnp.where(stat_id == per_dev, HQ, -1))
+    choose = (wanted == lax.broadcasted_iota(jnp.int32, (n * 8, LANES), 1)).astype(F32)
+    lse_tab[...] = jnp.dot(
+        choose, stats_t, precision=lax.Precision.HIGHEST, preferred_element_type=F32
+    ).reshape(lse_tab.shape)
     put = (
         lax.broadcasted_iota(jnp.int32, (pos, segs), 0) == owner_line + me
     ).astype(BF16)
-    for d in range(n):
-        scaled = jnp.concatenate(
-            [
-                (
-                    seg_out[:, pl.ds(head * HEAD_SIZE, HEAD_SIZE)] * weight[:, head : head + 1]
-                ).astype(BF16)
-                for head in range(d * per_dev, (d + 1) * per_dev)
-            ],
-            axis=1,
-        )
-        table[d] = jnp.dot(put, scaled, preferred_element_type=F32).astype(BF16)
-
-    cuts = [(pl.ds(r0, c), slice(None)) for r0, c in halves(pos, 16)]
+    for head in range(HQ):
+        cols = pl.ds(head * HEAD_SIZE, HEAD_SIZE)
+        seg_query[:, cols] = (seg_out[:, cols] * weight[:, head : head + 1]).astype(BF16)
+    for s, device in enumerate(places):
+        cols = pl.ds(pl.multiple_of(device * own_cols, own_cols), own_cols)
+        table[s // chips, s % chips] = jnp.dot(
+            put, seg_query[:, cols], preferred_element_type=F32
+        ).astype(BF16)
+
     scatter_sum(
         1,
         [
-            (table, table_sib, table_ring, cuts[0], 1),
-            (table, table_sib, table_ring, cuts[1], -1),
-            (lse_tab, lse_sib, lse_ring, every, 1),
+            (lse_tab, lse_sib, lse_ring, [(slice(None), slice(None))]),
+            (
+                table,
+                table_sib,
+                table_ring,
+                [(pl.ds(r0, c), slice(None)) for r0, c in halves(pos, 16)],
+            ),
         ],
     )
 
-    my_lse = lse_tab[me]
-    my_table = table[me]
+    my_lse = lse_tab[0, 0]
+    my_table = table[0, 0]
     row_of = my_lse[per_dev : per_dev + 1, :].astype(jnp.int32) - 1
-    hit = lax.broadcasted_iota(jnp.int32, (rows, pos_lanes), 0) == row_of
+    hit = row_ids((rows, pos_lanes), 0) == row_of
     heads = []
-    full = (slice(None), slice(None))
+    full = (slice(None), slice(None), slice(None))
     for h in range(per_dev):
         head = me * per_dev + h
         g = lax.div(head, group_size)
@@ -405,25 +429,21 @@
     def project(j, carry):
         cols = pl.ds(pl.multiple_of(j * tile, tile), tile)
         product = jnp.dot(attention, proj_v[:, cols], preferred_element_type=F32)
-        part[full + (cols,)] = product.astype(BF16).reshape(n, row_dev, tile)
+        part[full + (cols,)] = product.astype(BF16).reshape(2, chips, row_dev, tile)
         return carry
 
     lax.fori_loop(0, model // tile, project, 0)
     cuts = [(slice(None), pl.ds(c0, w)) for c0, w in halves(model, LANES)]
-    part_pieces = [
-        (part, part_sib, part_ring, cuts[0], 1),
-        (part, part_sib, part_ring, cuts[1], -1),
-    ]
-    scatter_sum(2, part_pieces)
+    scatter_sum(2, [(part, part_sib, part_ring, cuts)])
 
     loads[3].wait()
-    mixed = (hidden_v[...].astype(F32) + part[me].astype(F32)).astype(BF16).astype(F32)
+    mixed = (hidden_v[...].astype(F32) + part[0, 0].astype(F32)).astype(BF16).astype(F32)
     scale_row = lax.rsqrt(jnp.mean(mixed * mixed, axis=1, keepdims=True) + 1e-06)
-    normed_all[me] = (mixed * scale_row * gain_ref[...].astype(F32).reshape(1, model)).astype(BF16)
-    gather(3, [(normed_all, cuts[0], 1), (normed_all, cuts[1], -1)])
-
-    all_gates = gate_all[...].reshape(rows, LANES)
-    gate_lane = lax.broadcasted_iota(jnp.int32, (rows, LANES), 1)
+    normed_all[0, 0] = (mixed * scale_row * gain_ref[...].astype(F32).reshape(1, model)).astype(BF16)
+    gather(3, normed_all, cuts)
+
+    all_gates = gathered[full + (pl.ds(hd + 2 * kv_width, LANES),)].reshape(rows, LANES).astype(F32)
+    gate_lane = lax.rem(lax.broadcasted_iota(jnp.int32, (rows, LANES), 1), LANES // 2)
     gate = jnp.sum(jnp.where(gate_lane == me, all_gates, 0.0), axis=1, keepdims=True)
     loads[5].wait()
     loads[6].wait()
@@ -444,13 +464,13 @@
         cols = pl.ds(pl.multiple_of(j * tile, tile), tile)
         product = jnp.dot(act_v[...], wd_v[:, cols], preferred_element_type=F32)
         part[full + (cols,)] = (
-            (product * gate).astype(BF16).reshape(n, row_dev, tile)
+            (product * gate).astype(BF16).reshape(2, chips, row_dev, tile)
         )
         return carry
 
     lax.fori_loop(0, model // tile, down, 0)
-    scatter_sum(4, part_pieces)
-    out_ref[...] = (mixed + part[me].astype(F32)).astype(BF16)
+    scatter_sum(4, [(part, part_sib, part_ring, cuts)])
+    out_ref[...] = (mixed + part[0, 0].astype(F32)).astype(BF16)
 
 
 def on_device(
@@ -499,23 +519,22 @@
             pltpu.VMEM(w_down.shape[1:], BF16),
             pltpu.VMEM((row_dev, model), BF16),
             pltpu.SemaphoreType.DMA((8,)),
-            pltpu.VMEM((n, row_dev, hd + 2 * kv_width), BF16),
-            pltpu.VMEM((n, row_dev, LANES), F32),
+            pltpu.VMEM((2, chips, row_dev, hd + 2 * kv_width + LANES), BF16),
             pltpu.VMEM((segs, hd), BF16),
             pltpu.VMEM((segs, hd), F32),
-            pltpu.VMEM((n, pos, own_cols), BF16),
+            pltpu.VMEM((2, chips, pos, own_cols), BF16),
             pltpu.VMEM((chips, pos, own_cols), BF16),
             pltpu.VMEM((2, chips // 2, pos, own_cols), BF16),
-            pltpu.VMEM((n, 8, pos_lanes), F32),
+            pltpu.VMEM((2, chips, 8, pos_lanes), F32),
             pltpu.VMEM((chips, 8, pos_lanes), F32),
             pltpu.VMEM((2, chips // 2, 8, pos_lanes), F32),
-            pltpu.VMEM((n, row_dev, model), BF16),
+            pltpu.VMEM((2, chips, row_dev, model), BF16),
             pltpu.VMEM((chips, row_dev, model), BF16),
             pltpu.VMEM((2, chips // 2, row_dev, model), BF16),
-            pltpu.VMEM((n, row_dev, model), BF16),
+            pltpu.VMEM((2, chips, row_dev, model), BF16),
             pltpu.VMEM((rows, ff), BF16),
-            pltpu.SemaphoreType.DMA((5, 3, 2 * chips)),
-            pltpu.SemaphoreType.DMA((5, 3, 2 * chips)),
+            pltpu.SemaphoreType.DMA((5, 4, 4 + chips)),
+            pltpu.SemaphoreType.DMA((5, 4, 4 + chips)),
         ],
         compiler_params=pltpu.CompilerParams(
             collective_id=0, has_side_effects=True, vmem_limit_bytes=60 * 2**20

time: 112 us -> 114 us (1.018)
  Pallas kernels: 110 us -> 112 us
    pallas_call x1, Pallas kernels: 110 us -> 112 us  [on_device(): pl.pallas_call(functools.partial(layer_kernel, dims), out_shape=jax.Shape...]
where the time goes in v4:
time: 114 us
  Pallas kernels  112 us (98%)
  local copies, waits for them, and re-layouts  1.57 us (1%)
    pallas_call x1, Pallas kernels, on_device(): pl.pallas_call(functools.partial(layer_kernel, dims), out_shape=jax.Shape...  112 us

profile of v4, /device:TPU:0, one launch (start us, length us, event | category | flops | bytes accessed | tf_op | source)
XLA Modules:
  0.0 113.8 jit_solution(5967514954149915429)
XLA Ops:
  0.0 112.2 %decode_layer.1 = bf16[16,4096]{1,0:T(8,128)(2,1)} custom-call(bf16[16,4096]{1,0:T(8,128)(2,1)} %hidden_hbm.1, bf16[16,4096]{1,0:T(8,128)(2,1)} %query_hbm.1, bf16[16,2,256]{2,1,0:T(2,128)(2,1)} %fresh_ref.1, bf16[128,16,256]{2,1,0:T(8,128)(2,1)} %key_hbm.1, bf16[128,16,256]{2,1,0:T(8,128)(2,1)} %value_hbm.1, s32[1,128]{1,0:T(1,128)} %bitcast.6, ...), custom_call_target="tpu_custom_call" | custom-call | tf_op jit(solution)/shard_map/decode_layer/pallas_call | solution.py:508
  112.2 1.6 %copy.16 = bf16[16,4096]{1,0:T(8,128)(2,1)} copy(bf16[16,4096]{1,0:T(8,128)(2,1)} %decode_layer.1) | data formatting | bytes 262144

commit v5 on v4

--- a/solution.py
+++ b/solution.py
@@ -91,11 +91,11 @@
 
     sibling = chip * 2 + 1 - core
     beside = {d: chip_at(d) * 2 + core for d in (1, -1)}
+    across = {d: chip_at(d) * 2 + 1 - core for d in (1, -1)}
     near = list(range(1, reach - 1)) + [-dist for dist in range(reach - 2, 0, -1)]
-    far_away = [reach - 1, reach, 1 - reach]
-    offsets = [0] + near + far_away
+    offsets = [0] + near + [reach - 1, 1 - reach, reach]
     near_slots = pl.ds(1, len(near))
-    far_slots = pl.ds(1 + len(near), len(far_away))
+    far_slots = pl.ds(1 + len(near), 2)
     not_far = pl.ds(0, 1 + len(near))
 
     def slot_of(offset):
@@ -128,11 +128,12 @@
         ]
     ):
         copy = pltpu.make_async_copy(src, dst, load_sem.at[i])
-        copy.start()
+        if i < 5:
+            copy.start()
         loads.append(copy)
 
     barrier = pltpu.get_barrier_semaphore()
-    for other in (beside[1], beside[-1], sibling):
+    for other in (beside[1], beside[-1], across[1], across[-1], sibling):
         pl.semaphore_signal(
             barrier, inc=1, device_id={"dev": other}, device_id_type=pl.DeviceIdType.MESH
         )
@@ -176,13 +177,24 @@
                     )
                     ring[d, step, i] = copy
                     copies.append(copy)
+                    if step == reach - 1:
+                        copy = remote(
+                            buf.at[(0, slot_of(-d * step)) + cut],
+                            buf.at[(1, slot_of(reach)) + cut],
+                            phase,
+                            i,
+                            3,
+                            across[d],
+                        )
+                        copies.append(copy)
+                        beside_me.append(copy)
             if step == 0:
                 to_sibling(0, pl.ds(0, 1))
             if step == reach - 2:
                 to_sibling(1, near_slots)
+        to_sibling(2, far_slots)
         for i in range(len(cuts)):
             ring[1 - 2 * i, reach - 1, i].wait_recv()
-        to_sibling(2, far_slots)
         for copy in beside_me:
             copy.wait_recv()
         for copy in copies:
@@ -193,6 +205,29 @@
         ring = {}
         crossing = {}
         pieces = []
+        for a, (buf, sib, ring_in, cuts) in enumerate(arrays):
+            for i, cut in enumerate(cuts):
+                pieces.append((a, buf, sib, ring_in, cut, 2 * a + i, 1 - 2 * i))
+        for a, buf, sib, ring_in, cut, number, far in pieces:
+            side = 0 if far == 1 else 1
+            src = slot_of(reach)
+            ring[far, 0, number] = remote(
+                buf.at[(0, src) + cut],
+                ring_in.at[(side, 0) + cut],
+                phase,
+                number,
+                ring_slot(far, 0),
+                beside[far],
+            )
+            ring[0, 0, number] = remote(
+                buf.at[(1, src) + cut],
+                ring_in.at[(side, reach) + cut],
+                phase,
+                number,
+                3,
+                across[far],
+            )
+            copies += [ring[far, 0, number], ring[0, 0, number]]
         for a, (buf, sib, ring_in, cuts) in enumerate(arrays):
             for number, span in enumerate((far_slots, not_far)):
                 copy = remote(
@@ -200,25 +235,24 @@
                 )
                 copies.append(copy)
                 crossing[a, number] = copy
-            for i, cut in enumerate(cuts):
-                pieces.append((a, buf, sib, ring_in, cut, 2 * a + i, 1 - 2 * i))
 
         def crossed(a, number):
             if (a, number) in crossing:
                 crossing.pop((a, number)).wait_recv()
 
-        for step in range(reach):
+        for step in range(1, reach):
             for a, buf, sib, ring_in, cut, number, far in pieces:
                 crossed(a, 0 if step < 2 else 1)
                 for d in (1, -1):
-                    if step == 0 and far != d:
-                        continue
                     slot = slot_of(d * (reach - step))
                     where = (0, slot) + cut
                     total = buf[where].astype(F32) + sib[(slot,) + cut].astype(F32)
                     if (d, step - 1, number) in ring:
                         ring[d, step - 1, number].wait_recv()
                         total = total + ring_in[(0 if d == 1 else 1, step - 1) + cut].astype(F32)
+                    if step == 1 and d == far:
+                        ring[0, 0, number].wait_recv()
+                        total = total + ring_in[(0 if d == 1 else 1, reach) + cut].astype(F32)
                     buf[where] = total.astype(buf.dtype)
                     copy = remote(
                         buf.at[where],
@@ -255,8 +289,10 @@
         lane_id < LANES // 2, rounded, rest
     ).astype(BF16)
     loads[0].wait()
-    pl.semaphore_wait(barrier, 3)
+    pl.semaphore_wait(barrier, 5)
     gather(0, gathered, [(slice(None), pl.ds(c0, w)) for c0, w in halves(gathered.shape[-1], LANES)])
+    for copy in loads[5:]:
+        copy.start()
 
     owner_line = owner_ref[...]
     owner = jnp.broadcast_to(owner_line, (LANES, segs)).astype(F32).T.astype(jnp.int32)
@@ -524,13 +560,13 @@
             pltpu.VMEM((segs, hd), F32),
             pltpu.VMEM((2, chips, pos, own_cols), BF16),
             pltpu.VMEM((chips, pos, own_cols), BF16),
-            pltpu.VMEM((2, chips // 2, pos, own_cols), BF16),
+            pltpu.VMEM((2, chips // 2 + 1, pos, own_cols), BF16),
             pltpu.VMEM((2, chips, 8, pos_lanes), F32),
             pltpu.VMEM((chips, 8, pos_lanes), F32),
-            pltpu.VMEM((2, chips // 2, 8, pos_lanes), F32),
+            pltpu.VMEM((2, chips // 2 + 1, 8, pos_lanes), F32),
             pltpu.VMEM((2, chips, row_dev, model), BF16),
             pltpu.VMEM((chips, row_dev, model), BF16),
-            pltpu.VMEM((2, chips // 2, row_dev, model), BF16),
+            pltpu.VMEM((2, chips // 2 + 1, row_dev, model), BF16),
             pltpu.VMEM((2, chips, row_dev, model), BF16),
             pltpu.VMEM((rows, ff), BF16),
             pltpu.SemaphoreType.DMA((5, 4, 4 + chips)),

time: 114 us -> 112 us (0.982)
  Pallas kernels: 112 us -> 110 us
    pallas_call x1, Pallas kernels: 112 us -> 110 us  [on_device(): pl.pallas_call(functools.partial(layer_kernel, dims), out_shape=jax.Shape...]
where the time goes in v5:
time: 112 us
  Pallas kernels  110 us (98%)
  local copies, waits for them, and re-layouts  1.57 us (1%)
    pallas_call x1, Pallas kernels, on_device(): pl.pallas_call(functools.partial(layer_kernel, dims), out_shape=jax.Shape...  110 us

profile of v5, /device:TPU:0, one launch (start us, length us, event | category | flops | bytes accessed | tf_op | source)
XLA Modules:
  0.0 111.6 jit_solution(5279513887008951342)
XLA Ops:
  0.0 110.0 %decode_layer.1 = bf16[16,4096]{1,0:T(8,128)(2,1)} custom-call(bf16[16,4096]{1,0:T(8,128)(2,1)} %hidden_hbm.1, bf16[16,4096]{1,0:T(8,128)(2,1)} %query_hbm.1, bf16[16,2,256]{2,1,0:T(2,128)(2,1)} %fresh_ref.1, bf16[128,16,256]{2,1,0:T(8,128)(2,1)} %key_hbm.1, bf16[128,16,256]{2,1,0:T(8,128)(2,1)} %value_hbm.1, s32[1,128]{1,0:T(1,128)} %bitcast.6, ...), custom_call_target="tpu_custom_call" | custom-call | tf_op jit(solution)/shard_map/decode_layer/pallas_call | solution.py:544
  110.0 1.6 %copy.16 = bf16[16,4096]{1,0:T(8,128)(2,1)} copy(bf16[16,4096]{1,0:T(8,128)(2,1)} %decode_layer.1) | data formatting | bytes 262144

commit v6 on v5

--- a/solution.py
+++ b/solution.py
@@ -200,7 +200,7 @@
         for copy in copies:
             copy.wait_send()
 
-    def scatter_sum(phase, arrays):
+    def scatter_sum(phase, arrays, prepare=None):
         copies = []
         ring = {}
         crossing = {}
@@ -209,6 +209,8 @@
             for i, cut in enumerate(cuts):
                 pieces.append((a, buf, sib, ring_in, cut, 2 * a + i, 1 - 2 * i))
         for a, buf, sib, ring_in, cut, number, far in pieces:
+            if prepare is not None:
+                prepare(number)
             side = 0 if far == 1 else 1
             src = slot_of(reach)
             ring[far, 0, number] = remote(
@@ -228,21 +230,21 @@
                 across[far],
             )
             copies += [ring[far, 0, number], ring[0, 0, number]]
-        for a, (buf, sib, ring_in, cuts) in enumerate(arrays):
-            for number, span in enumerate((far_slots, not_far)):
+            for part_of, span in enumerate((far_slots, not_far)):
+                where = (span,) + cut
                 copy = remote(
-                    buf.at[1, span], sib.at[span], phase, 2 * a, number, sibling
+                    buf.at[(1,) + where], sib.at[where], phase, number, part_of, sibling
                 )
                 copies.append(copy)
-                crossing[a, number] = copy
-
-        def crossed(a, number):
-            if (a, number) in crossing:
-                crossing.pop((a, number)).wait_recv()
+                crossing[number, part_of] = copy
+
+        def crossed(number, part_of):
+            if (number, part_of) in crossing:
+                crossing.pop((number, part_of)).wait_recv()
 
         for step in range(1, reach):
             for a, buf, sib, ring_in, cut, number, far in pieces:
-                crossed(a, 0 if step < 2 else 1)
+                crossed(number, 0 if step < 2 else 1)
                 for d in (1, -1):
                     slot = slot_of(d * (reach - step))
                     where = (0, slot) + cut
@@ -468,9 +470,13 @@
         part[full + (cols,)] = product.astype(BF16).reshape(2, chips, row_dev, tile)
         return carry
 
-    lax.fori_loop(0, model // tile, project, 0)
     cuts = [(slice(None), pl.ds(c0, w)) for c0, w in halves(model, LANES)]
-    scatter_sum(2, [(part, part_sib, part_ring, cuts)])
+    half_tiles = model // tile // 2
+
+    def project_half(i):
+        lax.fori_loop(i * half_tiles, (i + 1) * half_tiles, project, 0)
+
+    scatter_sum(2, [(part, part_sib, part_ring, cuts)], project_half)
 
     loads[3].wait()
     mixed = (hidden_v[...].astype(F32) + part[0, 0].astype(F32)).astype(BF16).astype(F32)
@@ -504,8 +510,10 @@
         )
         return carry
 
-    lax.fori_loop(0, model // tile, down, 0)
-    scatter_sum(4, [(part, part_sib, part_ring, cuts)])
+    def down_half(i):
+        lax.fori_loop(i * half_tiles, (i + 1) * half_tiles, down, 0)
+
+    scatter_sum(4, [(part, part_sib, part_ring, cuts)], down_half)
     out_ref[...] = (mixed + part[0, 0].astype(F32)).astype(BF16)
 
 

time: 112 us -> 109 us (0.973)
  Pallas kernels: 110 us -> 107 us
    pallas_call x1, Pallas kernels: 110 us -> 107 us  [on_device(): pl.pallas_call(functools.partial(layer_kernel, dims), out_shape=jax.Shape...]
where the time goes in v6:
time: 109 us
  Pallas kernels  107 us (98%)
  local copies, waits for them, and re-layouts  1.57 us (1%)
    pallas_call x1, Pallas kernels, on_device(): pl.pallas_call(functools.partial(layer_kernel, dims), out_shape=jax.Shape...  107 us

profile of v6, /device:TPU:0, one launch (start us, length us, event | category | flops | bytes accessed | tf_op | source)
XLA Modules:
  0.0 109.0 jit_solution(9570918146389927589)
XLA Ops:
  0.0 107.5 %decode_layer.1 = bf16[16,4096]{1,0:T(8,128)(2,1)} custom-call(bf16[16,4096]{1,0:T(8,128)(2,1)} %hidden_hbm.1, bf16[16,4096]{1,0:T(8,128)(2,1)} %query_hbm.1, bf16[16,2,256]{2,1,0:T(2,128)(2,1)} %fresh_ref.1, bf16[128,16,256]{2,1,0:T(8,128)(2,1)} %key_hbm.1, bf16[128,16,256]{2,1,0:T(8,128)(2,1)} %value_hbm.1, s32[1,128]{1,0:T(1,128)} %bitcast.6, ...), custom_call_target="tpu_custom_call" | custom-call | tf_op jit(solution)/shard_map/decode_layer/pallas_call | solution.py:552
  107.5 1.6 %copy.16 = bf16[16,4096]{1,0:T(8,128)(2,1)} copy(bf16[16,4096]{1,0:T(8,128)(2,1)} %decode_layer.1) | data formatting | bytes 262144
